TPU v7x, 128 devices: a whole 4x4x4 slice. The times are simulated.
128 devices in a mesh: rep: 4 (over x_hi, core), shard: 32 (over y, x_lo, z).
Axes of the slice: x: 4 (x_hi: 2, x_lo: 2; x = x_hi * 2 + x_lo), y: 4, z: 4, core: 2. Of those that a mesh axis runs over, the one named last changes fastest.
Arguments:
- hidden: bfloat16 [32768, 8192], P(('rep', 'shard')), may hold values from -6 to 6
- seg_ids: int32 [128, 256], P(('rep', 'shard')), may hold values from 0 to 15, never falling along the last dimension, each value on 1 to 32 neighbouring positions
- ranks: int32 [128, 2, 8], P(('rep', 'shard')), may hold values from 0 to 7, each once within a row
- adapter_in: bfloat16 [3, 8192, 128], P(None, 'shard'), may hold values from -0.0625 to 0.0625
- adapter_out: bfloat16 [3, 128, 8192], P(None, None, 'shard'), may hold values from -0.5 to 0.5
- score_head: bfloat16 [8192], P('shard'), may hold values from -0.25 to 0.25
- final_gain: bfloat16 [8192], P('shard'), may hold values from 0.5 to 1.5
Outputs:
- grad_in: float32 [3, 8192, 128], P(None, 'shard')
- grad_out: float32 [3, 128, 8192], P(None, None, 'shard')
- grad_head: float32 [8192], P('shard')
- grad_gain: float32 [8192], P('shard')
Inputs may be any that keep to these rules, and one draw needn't show every extreme that they name: Each row of ranks orders the 8 responses of one list, best first.
All inputs are finite; a program needn't handle non-finite values.
Results may differ from a plain program's by a relative error of at most 0.034.
Values may be sent and summed in bfloat16 or wider, within the bound.
A program may use at most 128 MiB of HBM per device.

v0:
```python
import jax
import jax.numpy as jnp
from jax import lax
from jax.sharding import PartitionSpec as P

EPS = 1e-06


def norm_rows(values):
    rinv = lax.rsqrt(jnp.mean(values * values, axis=-1, keepdims=True) + EPS)
    return (values * rinv, rinv)


def layer_forward(state, w_in, w_out):
    values = state.astype(jnp.float32)
    normed, rinv = norm_rows(values)
    unit = normed.astype(jnp.bfloat16)
    inner = jnp.dot(unit, w_in, preferred_element_type=jnp.float32)
    active = jax.nn.silu(inner).astype(jnp.bfloat16)
    outer = jnp.dot(active, w_out, preferred_element_type=jnp.float32)
    return ((values + outer).astype(jnp.bfloat16), (state, unit, inner, active))


def layer_backward(upper, saved, w_in, w_out):
    state, unit, inner, active = saved
    normed, rinv = norm_rows(state.astype(jnp.float32))
    grad_b = lax.dot_general(
        active, upper, (((0,), (0,)), ((), ())), preferred_element_type=jnp.float32
    )
    d_active = lax.dot_general(
        upper, w_out, (((1,), (1,)), ((), ())), preferred_element_type=jnp.float32
    )
    sigm = jax.nn.sigmoid(inner)
    d_inner = (d_active * sigm * (1.0 + inner * (1.0 - sigm))).astype(jnp.bfloat16)
    grad_a = lax.dot_general(
        d_inner, unit, (((0,), (0,)), ((), ())), preferred_element_type=jnp.float32
    )
    d_unit = lax.dot_general(
        d_inner, w_in, (((1,), (1,)), ((), ())), preferred_element_type=jnp.float32
    )
    d_state = rinv * (d_unit - normed * jnp.mean(d_unit * normed, axis=-1, keepdims=True))
    lower = (upper.astype(jnp.float32) + d_state).astype(jnp.bfloat16)
    return (lower, grad_a, grad_b)


def head_backward(state, segment, order, head, gain):
    n_lists = order.shape[0]
    n_resp = order.shape[1]
    values = state.astype(jnp.float32)
    normed, rinv = norm_rows(values)
    gain_f = gain.astype(jnp.float32)
    head_f = head.astype(jnp.float32)
    feats = normed * gain_f[None, :]
    n_segs = n_lists * n_resp
    onehot = (segment[None, :] == jnp.arange(n_segs, dtype=jnp.int32)[:, None]).astype(jnp.float32)
    counts = jnp.sum(onehot, axis=1)
    pooled = jnp.dot(onehot, feats, precision=lax.Precision.HIGHEST) / counts[:, None]
    reward = jnp.dot(pooled, head_f, precision=lax.Precision.HIGHEST).reshape(n_lists, n_resp)
    select = (order[:, :, None] == jnp.arange(n_resp, dtype=jnp.int32)[None, None, :]).astype(
        jnp.float32
    )
    placed = jnp.sum(select * reward[:, None, :], axis=-1)
    expo = jnp.exp(placed)
    suffix = jnp.flip(jnp.cumsum(jnp.flip(expo, -1), axis=-1), -1)
    prefix = jnp.cumsum(1.0 / suffix, axis=-1)
    d_placed = -1.0 + expo * prefix
    d_reward = jnp.sum(select * d_placed[:, :, None], axis=1).reshape(n_segs)
    grad_head = jnp.dot(d_reward, pooled, precision=lax.Precision.HIGHEST)
    coeff = jnp.dot(d_reward / counts, onehot, precision=lax.Precision.HIGHEST)
    d_feats = coeff[:, None] * head_f[None, :]
    grad_gain = jnp.sum(d_feats * normed, axis=0)
    d_normed = d_feats * gain_f[None, :]
    d_state = rinv * (d_normed - normed * jnp.mean(d_normed * normed, axis=-1, keepdims=True))
    return (d_state.astype(jnp.bfloat16), grad_head, grad_gain)


def body(hidden, seg_ids, ranks, adapter_in, adapter_out, score_head, final_gain):
    n_layers = adapter_in.shape[0]
    state = hidden
    kept = []
    weights_in = []
    weights_out = []
    for layer in range(n_layers):
        if layer == 0:
            w_in, w_out, head, gain = (
                lax.all_gather(adapter_in[0], "shard", axis=0, tiled=True),
                lax.all_gather(adapter_out[0], "shard", axis=1, tiled=True),
                lax.all_gather(score_head, "shard", axis=0, tiled=True),
                lax.all_gather(final_gain, "shard", axis=0, tiled=True),
            )
        else:
            w_in, w_out = (
                lax.all_gather(adapter_in[layer], "shard", axis=0, tiled=True),
                lax.all_gather(adapter_out[layer], "shard", axis=1, tiled=True),
            )
        weights_in.append(w_in)
        weights_out.append(w_out)
        state, saved = layer_forward(state, w_in, w_out)
        kept.append(saved)
    upper, g_head, g_gain = head_backward(state, seg_ids[0], ranks[0], head, gain)
    extras = jnp.stack([g_head, g_gain])
    parts_a = []
    parts_b = []
    for layer in range(n_layers - 1, -1, -1):
        upper, grad_a, grad_b = layer_backward(
            upper, kept[layer], weights_in[layer], weights_out[layer]
        )
        if layer == n_layers - 1:
            red_a, red_b, red_x = (
                lax.psum_scatter(
                    grad_a.astype(jnp.bfloat16), "shard", scatter_dimension=1, tiled=True
                ).astype(jnp.float32),
                lax.psum_scatter(
                    grad_b.astype(jnp.bfloat16), "shard", scatter_dimension=1, tiled=True
                ).astype(jnp.float32),
                lax.psum_scatter(
                    extras.astype(jnp.bfloat16), "shard", scatter_dimension=1, tiled=True
                ).astype(jnp.float32),
            )
        else:
            red_a, red_b = (
                lax.psum_scatter(
                    grad_a.astype(jnp.bfloat16), "shard", scatter_dimension=1, tiled=True
                ).astype(jnp.float32),
                lax.psum_scatter(
                    grad_b.astype(jnp.bfloat16), "shard", scatter_dimension=1, tiled=True
                ).astype(jnp.float32),
            )
        parts_a.append(red_a)
        parts_b.append(red_b)
    stack_a = jnp.stack(parts_a[::-1])
    stack_b = jnp.stack(parts_b[::-1])
    sum_a, sum_b, sum_x = lax.psum((stack_a, stack_b, red_x), "rep")
    return (jnp.transpose(sum_a, (0, 2, 1)), sum_b, sum_x[0], sum_x[1])


def solution(mesh):
    placed = (
        P(("rep", "shard"), None),
        P(("rep", "shard"), None),
        P(("rep", "shard"), None, None),
        P(None, "shard", None),
        P(None, None, "shard"),
        P("shard"),
        P("shard"),
    )
    return jax.shard_map(
        body,
        mesh=mesh,
        in_specs=placed,
        out_specs=(P(None, "shard", None), P(None, None, "shard"), P("shard"), P("shard")),
        check_vma=False,
    )
```

profile of v0, /device:TPU:1, one launch (start us, length us, event | category | flops | bytes accessed | tf_op | source)
XLA Modules:
  0.0 2064.7 jit_solution(5468414077508512083)
XLA Ops:
  14.3 69.8 %all-gather.7 = bf16[32,1,256]{2,1,0:T(2,128)(2,1)S(1)} all-gather(bf16[1,1,256]{2,1,0:T(2,128)(2,1)S(1)} %reshape.81), channel_id=1, replica_groups=mesh['rep'=4,'shard'=32] {'shard'}, dimensions={0}, use_global_device_ids=true | all-gather | bytes 16896 | tf_op jit(solution)/shard_map/all_gather | solution.py:88
  84.2 62.2 %all-gather.6 = bf16[32,1,256]{2,1,0:T(2,128)(2,1)S(1)} all-gather(bf16[1,1,256]{2,1,0:T(2,128)(2,1)S(1)} %reshape.79), channel_id=1, replica_groups=mesh['rep'=4,'shard'=32] {'shard'}, dimensions={0}, use_global_device_ids=true | all-gather | bytes 16896 | tf_op jit(solution)/shard_map/all_gather | solution.py:89
  154.5 122.8 %all-gather.17.cloned.1.call-done = bf16[1,128,8192]{2,1,0:T(8,128)(2,1)} async-done(((bf16[1,128,256]{2,1,0:T(8,128)(2,1)}), bf16[1,128,8192]{2,1,0:T(8,128)(2,1)}) %all-gather.17.cloned.1.call-update) | async-done | bytes 2097168 | tf_op jit(solution)/shard_map/all_gather | solution.py:87
  277.3 6.4 fusion.31
  283.7 142.9 %all-gather.19.cloned.1.call-done = bf16[1,8192,128]{2,1,0:T(8,128)(2,1)} async-done(((bf16[1,256,128]{2,1,0:T(8,128)(2,1)}), bf16[1,8192,128]{2,1,0:T(8,128)(2,1)}) %all-gather.19.cloned.1.call-update) | async-done | bytes 2097168 | tf_op jit(solution)/shard_map/all_gather | solution.py:93
  430.8 127.0 %all-gather.21.cloned.1.call-done = bf16[1,128,8192]{2,1,0:T(8,128)(2,1)} async-done(((bf16[1,128,256]{2,1,0:T(8,128)(2,1)}), bf16[1,128,8192]{2,1,0:T(8,128)(2,1)}) %all-gather.21.cloned.1.call-update) | async-done | bytes 2097168 | tf_op jit(solution)/shard_map/all_gather | solution.py:94
  557.8 6.4 fusion.32
  564.2 142.7 %all-gather.23.cloned.1.call-done = bf16[1,8192,128]{2,1,0:T(8,128)(2,1)} async-done(((bf16[1,256,128]{2,1,0:T(8,128)(2,1)}), bf16[1,8192,128]{2,1,0:T(8,128)(2,1)}) %all-gather.23.cloned.1.call-update) | async-done | bytes 2097168 | tf_op jit(solution)/shard_map/all_gather | solution.py:93
  711.1 127.6 %all-gather.25.cloned.1.call-done = bf16[1,128,8192]{2,1,0:T(8,128)(2,1)} async-done(((bf16[1,128,256]{2,1,0:T(8,128)(2,1)}), bf16[1,128,8192]{2,1,0:T(8,128)(2,1)}) %all-gather.25.cloned.1.call-update) | async-done | bytes 2097168 | tf_op jit(solution)/shard_map/all_gather | solution.py:94
  838.6 4.6 fusion.14
  848.6 5.0 fusion.28
  867.7 5.1 fusion.19
  888.1 7.8 convolution_convert_fusion.5
  896.0 4.3 convolution_convert_fusion
  900.6 4.3 convolution_convert_fusion.1
  912.0 105.2 %reduce-scatter.14.cloned.1.call-done = bf16[128,256]{1,0:T(8,128)(2,1)} async-done(((bf16[128,8192]{1,0:T(8,128)(2,1)}), bf16[128,256]{1,0:T(8,128)(2,1)}) %reduce-scatter.14.cloned.1.call-update) | async-done | bytes 65552 | tf_op jit(solution)/shard_map/reduce_scatter | solution.py:110
  1017.1 161.5 %reduce-scatter.12.cloned.1.call-done = bf16[128,256]{1,0:T(8,128)(2,1)} async-done(((bf16[128,8192]{1,0:T(8,128)(2,1)}), bf16[128,256]{1,0:T(8,128)(2,1)}) %reduce-scatter.12.cloned.1.call-update) | async-done | bytes 65552 | tf_op jit(solution)/shard_map/reduce_scatter | solution.py:122
  1178.6 162.7 %reduce-scatter.10.cloned.1.call-done = bf16[128,256]{1,0:T(8,128)(2,1)} async-done(((bf16[128,8192]{1,0:T(8,128)(2,1)}), bf16[128,256]{1,0:T(8,128)(2,1)}) %reduce-scatter.10.cloned.1.call-update) | async-done | bytes 65552 | tf_op jit(solution)/shard_map/reduce_scatter | solution.py:122
  1343.0 159.8 %reduce-scatter.20.cloned.1.call-done = bf16[128,256]{1,0:T(8,128)(2,1)} async-done(((bf16[128,8192]{1,0:T(8,128)(2,1)}), bf16[128,256]{1,0:T(8,128)(2,1)}) %reduce-scatter.20.cloned.1.call-update) | async-done | bytes 65552 | tf_op jit(solution)/shard_map/reduce_scatter | solution.py:113
  1502.8 161.5 %reduce-scatter.18.cloned.1.call-done = bf16[128,256]{1,0:T(8,128)(2,1)} async-done(((bf16[128,8192]{1,0:T(8,128)(2,1)}), bf16[128,256]{1,0:T(8,128)(2,1)}) %reduce-scatter.18.cloned.1.call-update) | async-done | bytes 65552 | tf_op jit(solution)/shard_map/reduce_scatter | solution.py:125
  1664.3 161.5 %reduce-scatter.16.cloned.1.call-done = bf16[128,256]{1,0:T(8,128)(2,1)} async-done(((bf16[128,8192]{1,0:T(8,128)(2,1)}), bf16[128,256]{1,0:T(8,128)(2,1)}) %reduce-scatter.16.cloned.1.call-update) | async-done | bytes 65552 | tf_op jit(solution)/shard_map/reduce_scatter | solution.py:125
  1827.5 159.8 %reduce-scatter.22.cloned.1.call-done = bf16[256,2]{1,0:T(8,128)(2,1)} async-done(((bf16[8192,2]{1,0:T(8,128)(2,1)}), bf16[256,2]{1,0:T(8,128)(2,1)}) %reduce-scatter.22.cloned.1.call-update) | async-done | bytes 1040
  1988.2 31.1 %psum.23 = f32[2,256]{1,0:T(2,128)S(1)} all-reduce(bf16[2,256]{1,0:T(2,128)(2,1)S(1)} %copy.16), channel_id=1, replica_groups=mesh['rep'=4,'shard'=32] {'rep'}, use_global_device_ids=true, to_apply=%region_22.23 | all-reduce | flops 512 | bytes 3072 | tf_op jit(solution)/shard_map/psum | solution.py:133
  2019.9 34.7 %all-reduce.3.cloned.1.call-done = (f32[3,256,128]{1,2,0:T(8,128)}, f32[3,128,256]{2,1,0:T(8,128)}) async-done(((f32[3,256,128]{1,2,0:T(8,128)}, f32[3,128,256]{2,1,0:T(8,128)}), (f32[3,256,128]{1,2,0:T(8,128)}, f32[3,128,256]{2,1,0:T(8,128)})) %all-reduce.3.cloned.1.call-update) | async-done | bytes 786448 | tf_op jit(solution)/shard_map/psum | solution.py:133
  (119 shorter events, 74.1 us)
Async XLA Ops:
  7.2 143.2 %all-gather.15.cloned.1.call-start = ((), (), s32[]{:S(2)}) async-start(), calls=%async_computation.13 | async-start | bytes 2162688 | tf_op jit(solution)/shard_map/all_gather | solution.py:86
  8.8 268.5 %all-gather.17.cloned.1.call-start = ((), (), s32[]{:S(2)}) async-start(), calls=%async_computation.14 | async-start | bytes 2162688 | tf_op jit(solution)/shard_map/all_gather | solution.py:87
  10.5 416.1 %all-gather.19.cloned.1.call-start = ((), (), s32[]{:S(2)}) async-start(), calls=%async_computation.15 | async-start | bytes 2162688 | tf_op jit(solution)/shard_map/all_gather | solution.py:93
  11.2 546.6 %all-gather.21.cloned.1.call-start = ((), (), s32[]{:S(2)}) async-start(), calls=%async_computation.16 | async-start | bytes 2162688 | tf_op jit(solution)/shard_map/all_gather | solution.py:94
  11.8 695.1 %all-gather.23.cloned.1.call-start = ((), (), s32[]{:S(2)}) async-start(), calls=%async_computation.17 | async-start | bytes 2162688 | tf_op jit(solution)/shard_map/all_gather | solution.py:93
  12.4 826.3 %all-gather.25.cloned.1.call-start = ((), (), s32[]{:S(2)}) async-start(), calls=%async_computation.18 | async-start | bytes 2162688 | tf_op jit(solution)/shard_map/all_gather | solution.py:94
  12.9 1004.2 %reduce-scatter.14.cloned.1.call-start = ((), (), s32[]{:S(2)}) async-start(), calls=%async_computation.9 | async-start | bytes 2162688 | tf_op jit(solution)/shard_map/reduce_scatter | solution.py:110
  711.1 132.2 %copy-start.16 = (s32[1,256]{1,0:T(1,128)S(1)}, s32[1,256]{1,0:T(1,128)}, u32[]{:S(2)}) copy-start(s32[1,256]{1,0:T(1,128)} %param.8) | copy-start | bytes 3076
  843.2 3.8 copy-start.4
  843.2 4.3 copy-start.15
  848.4 5.2 copy-start.5
  853.6 4.5 copy-start.14
  862.9 315.8 %reduce-scatter.12.cloned.1.call-start = ((), (), s32[]{:S(2)}) async-start(), calls=%async_computation.8 | async-start | bytes 2162688 | tf_op jit(solution)/shard_map/reduce_scatter | solution.py:122
  862.9 4.7 copy-start.6
  867.6 7.0 copy-start.12
  879.4 461.9 %reduce-scatter.10.cloned.1.call-start = ((), (), s32[]{:S(2)}) async-start(), calls=%async_computation.7 | async-start | bytes 2162688 | tf_op jit(solution)/shard_map/reduce_scatter | solution.py:122
  879.5 3.7 copy-start.1
  879.5 4.7 copy-start.8
  884.2 3.9 copy-start.10
  895.9 606.9 %reduce-scatter.20.cloned.1.call-start = ((), (), s32[]{:S(2)}) async-start(), calls=%async_computation.12 | async-start | bytes 2162688 | tf_op jit(solution)/shard_map/reduce_scatter | solution.py:113
  900.3 764.0 %reduce-scatter.18.cloned.1.call-start = ((), (), s32[]{:S(2)}) async-start(), calls=%async_computation.11 | async-start | bytes 2162688 | tf_op jit(solution)/shard_map/reduce_scatter | solution.py:125
  904.9 920.9 %reduce-scatter.16.cloned.1.call-start = ((), (), s32[]{:S(2)}) async-start(), calls=%async_computation.10 | async-start | bytes 2162688 | tf_op jit(solution)/shard_map/reduce_scatter | solution.py:125
  909.3 1078.0 %reduce-scatter.22.cloned.1.call-start = ((), (), s32[]{:S(2)}) async-start(), calls=%async_computation.19 | async-start | bytes 2162688
  911.9 1142.6 %all-reduce.3.cloned.1.call-start = ((), (), s32[]{:S(2)}) async-start(), calls=%async_computation.20 | async-start | bytes 1572864 | tf_op jit(solution)/shard_map/psum | solution.py:133
  (7 other events, 17.2 us)
Sparse Core Ops, SparseCore 0:
  9.6 135.8 all-gather.14
  147.7 129.5 all-gather.16
  279.0 147.5 all-gather.18
  428.0 129.6 all-gather.20
  559.3 147.5 all-gather.22
  708.9 129.7 all-gather.24
  863.0 154.0 reduce-scatter.13
  1019.6 158.9 reduce-scatter.11
  1181.0 160.2 reduce-scatter.9
  1343.7 159.0 reduce-scatter.19
  1505.2 159.0 reduce-scatter.17
  1666.7 159.0 reduce-scatter.15
  1828.2 159.0 reduce-scatter.21
  1990.4 64.0 all-reduce.2
where the time goes:
time: 2070 us; the launch traced here: 2060 us
  waiting for transfers between devices  1770 us (86%)
  blocking collectives  163 us (8%)
  matrix products  70.2 us (3%)
  other arithmetic  24.7 us (1%)
    reduce_scatter x3, waiting for transfers between devices, body(): lax.psum_scatter(grad_b.astype(jnp.bfloat16), 'shard', scatter_dimension=...  483 us
    reduce_scatter x3, waiting for transfers between devices, body(): lax.psum_scatter(grad_a.astype(jnp.bfloat16), 'shard', scatter_dimension=...  429 us
    all_gather x2, waiting for transfers between devices, body(): lax.all_gather(adapter_in[layer], 'shard', axis=0, tiled=True)  286 us
    all_gather x2, waiting for transfers between devices, body(): lax.all_gather(adapter_out[layer], 'shard', axis=1, tiled=True)  255 us
    unnamed x15, waiting for transfers between devices  162 us
    all_gather x1, waiting for transfers between devices, body(): lax.all_gather(adapter_out[0], 'shard', axis=1, tiled=True)  123 us
    all_gather x1, blocking collectives, body(): lax.all_gather(score_head, 'shard', axis=0, tiled=True)  69.8 us
    all_gather x1, blocking collectives, body(): lax.all_gather(final_gain, 'shard', axis=0, tiled=True)  62.2 us
  transfers between devices with their start and end apart: 14, of which 13 were waited for; matrix products, arithmetic and copies ran while one was open for 4% of the time, Pallas kernels for 0%

commit v1 on v0

v1 whole, which is shorter than its diff:
```python
import jax
import jax.numpy as jnp
from jax import lax
from jax.experimental import pallas as pl
from jax.experimental.pallas import tpu as pltpu
from jax.sharding import PartitionSpec as P

EPS = 1e-06
MESH = pl.DeviceIdType.MESH
F32 = jnp.float32
BF16 = jnp.bfloat16
LAYERS = 3
WIDTH = 8192
TOK = 256
ROWS = 2 * TOK
R = 128
HALF = 128
EXTRA = 16
N_SEMS = 192
NT = (((1,), (1,)), ((), ()))
CHUNK = 256


def unit_rows(layer):
    return R + EXTRA if layer == LAYERS - 1 else R


def scratch():
    shapes = {}
    for level in range(LAYERS + 1):
        shapes["h", level] = pltpu.VMEM((4, 4, ROWS, 2 * HALF), BF16)
        shapes["sq", level] = pltpu.VMEM((ROWS, 128), F32)
        shapes["sq_in", level] = pltpu.VMEM((ROWS, 128), F32)
        shapes["rinv", level] = pltpu.VMEM((ROWS, 128), F32)
    for layer in range(LAYERS):
        rows = unit_rows(layer)
        shapes["own", layer] = pltpu.VMEM((rows, HALF), BF16)
        shapes["wa", layer] = pltpu.VMEM((4, 4, 2, HALF, R), BF16)
        shapes["wb", layer] = pltpu.VMEM((2, 4, 4, rows, HALF), BF16)
        shapes["z", layer] = pltpu.VMEM((ROWS, R), F32)
        shapes["z_in", layer] = pltpu.VMEM((ROWS, R), F32)
        shapes["act_t", layer] = pltpu.VMEM((R, ROWS), BF16)
        shapes["da", layer] = pltpu.VMEM((ROWS, R), F32)
        shapes["da_in", layer] = pltpu.VMEM((ROWS, R), F32)
        shapes["ga", layer] = pltpu.VMEM((2, 4, 4, R, HALF), BF16)
        shapes["ga1", layer] = pltpu.VMEM((2, 4, R, HALF), BF16)
        shapes["ga2", layer] = pltpu.VMEM((2, 2, 4, R, HALF), BF16)
        shapes["ga3", layer] = pltpu.VMEM((2, R, HALF), BF16)
        shapes["ga4", layer] = pltpu.VMEM((2, 2, R, HALF), BF16)
        shapes["ga5", layer] = pltpu.VMEM((R, HALF), BF16)
        shapes["ga6", layer] = pltpu.VMEM((2, 2, R, HALF), F32)
        shapes["gb", layer] = pltpu.VMEM((2, 4, 4, rows, HALF), BF16)
        shapes["gb1", layer] = pltpu.VMEM((4, 4, rows, HALF), BF16)
        shapes["gb2", layer] = pltpu.VMEM((4, rows, HALF), BF16)
        shapes["gb3", layer] = pltpu.VMEM((2, 4, rows, HALF), BF16)
        shapes["gb4", layer] = pltpu.VMEM((rows, HALF), BF16)
        shapes["gb5", layer] = pltpu.VMEM((2, rows, HALF), BF16)
        shapes["gb6", layer] = pltpu.VMEM((2, 2, rows, HALF), F32)
    shapes["act"] = pltpu.VMEM((ROWS, R), BF16)
    shapes["dzr"] = pltpu.VMEM((ROWS, R), BF16)
    shapes["dzr_t"] = pltpu.VMEM((R, ROWS), BF16)
    shapes["tok"] = pltpu.VMEM((ROWS, 128), F32)
    shapes["q"] = pltpu.VMEM((ROWS, 128), F32)
    shapes["q_in"] = pltpu.VMEM((ROWS, 128), F32)
    shapes["coef"] = pltpu.VMEM((ROWS, 128), F32)
    shapes["vec"] = pltpu.VMEM((16, ROWS), BF16)
    shapes["hg"] = pltpu.VMEM((4, 4, 8, 2 * HALF), F32)
    shapes["packs"] = pltpu.VMEM((2, 8, 256), F32)
    shapes["send"] = pltpu.SemaphoreType.DMA((N_SEMS,))
    shapes["recv"] = pltpu.SemaphoreType.DMA((N_SEMS,))
    shapes["local"] = pltpu.SemaphoreType.DMA((16,))
    return shapes


def kernel(hidden, w_in, w_out, pack, grad_in, grad_out, grad_vec, *refs):
    s = dict(zip(scratch(), refs))
    rep, shard = lax.axis_index("rep"), lax.axis_index("shard")
    xh, c = rep // 2, rep % 2
    y, xl, z = shard // 8, (shard // 4) % 2, shard % 4
    other = 1 - c
    p, q = y * other + z * c, z * other + y * c
    pp, p2, pm = (p + 1) % 4, (p + 2) % 4, (p + 3) % 4
    qp, q2, qm = (q + 1) % 4, (q + 2) % 4, (q + 3) % 4

    def at(y_by, z_by):
        return (rep, (y + y_by) % 4 * 8 + xl * 4 + (z + z_by) % 4)

    def along_x(by):
        x = (xh * 2 + xl + by) % 4
        return (x // 2 * 2 + c, y * 8 + x % 2 * 4 + z)

    to_pp, to_pm = at(other, c), at(3 * other, 3 * c)
    to_qp, to_qm = at(c, other), at(3 * c, 3 * other)
    to_xp, to_xm = along_x(1), along_x(3)
    to_pair = (rep, y * 8 + (1 - xl) * 4 + z)
    to_core = (xh * 2 + other, shard)
    to_rep = ((1 - xh) * 2 + c, shard)
    to_both = ((1 - xh) * 2 + other, shard)

    used = [0, 0]
    started = []

    def send(src, dst, to):
        i = used[0]
        used[0] += 1
        copy = pltpu.make_async_remote_copy(
            src_ref=src,
            dst_ref=dst,
            send_sem=s["send"].at[i],
            recv_sem=s["recv"].at[i],
            device_id=to,
            device_id_type=MESH,
        )
        copy.start()
        started.append(copy)
        return copy

    def local(src, dst):
        copy = pltpu.make_async_copy(src, dst, s["local"].at[used[1]])
        used[1] += 1
        copy.start()
        return copy

    def arrived(*copies):
        for copy in copies:
            copy.wait_recv()

    mine = pl.ds(pl.multiple_of(c * HALF, HALF), HALF)
    my_rows = pl.ds(pl.multiple_of(c * TOK, TOK), TOK)
    their_rows = pl.ds(pl.multiple_of(other * TOK, TOK), TOK)
    local_in = [
        local(w_in.at[l, mine], s["wa", l].at[p, q, xl]) for l in range(LAYERS)
    ]
    local_out = [
        local(w_out.at[l, :, mine], s["own", l].at[pl.ds(0, R)]) for l in range(LAYERS)
    ]

    barrier = pltpu.get_barrier_semaphore()
    partners = (to_pp, to_pm, to_qp, to_qm, to_xp, to_xm, to_core, to_rep, to_both)
    for partner in partners:
        pl.semaphore_signal(barrier, inc=1, device_id=partner, device_id_type=MESH)

    hidden_sem = s["local"].at[15]

    def load_hidden(i, carry):
        yy, zz = i // 4, i % 4
        for xx in range(2):
            col = pl.multiple_of(yy * 2048 + xx * 1024 + zz * 256 + c * HALF, HALF)
            pltpu.make_async_copy(
                hidden.at[:, pl.ds(col, HALF)],
                s["h", 0].at[yy * other + zz * c, zz * other + yy * c, my_rows, pl.ds(xx * HALF, HALF)],
                hidden_sem,
            ).start()
        return carry

    lax.fori_loop(0, 16, load_hidden, 0)
    pl.semaphore_wait(barrier, len(partners))

    def gather_in(l):
        w = s["wa", l]
        a = send(w_in.at[l, mine], w.at[p, q, xl], to_pair)
        yield
        local_in[l].wait()
        arrived(a)
        a = send(w.at[p, q], w.at[p, q], to_qp)
        b = send(w.at[p, q], w.at[p, q], to_qm)
        yield
        arrived(a, b)
        a = send(w.at[p, qm, 0], w.at[p, qm, 0], to_qp)
        b = send(w.at[p, qp, 1], w.at[p, qp, 1], to_qm)
        yield
        arrived(a, b)
        a = send(w.at[p], w.at[p], to_pp)
        b = send(w.at[p], w.at[p], to_pm)
        yield
        arrived(a, b)
        a = send(w.at[pm, pl.ds(0, 2)], w.at[pm, pl.ds(0, 2)], to_pp)
        b = send(w.at[pp, pl.ds(2, 2)], w.at[pp, pl.ds(2, 2)], to_pm)
        yield
        arrived(a, b)
        yield

    def gather_out(l):
        w, own, rows = s["wb", l], s["own", l], unit_rows(l)
        low, high = pl.ds(0, 64), pl.ds(64, rows - 64)
        local_out[l].wait()
        if rows > R:
            head, gain = pack[0:1, :], pack[1:2, :]
            both = head * gain
            both = both[:, :HALF] * (1 - c).astype(F32) + both[:, HALF:] * c.astype(F32)
            hi = both.astype(BF16)
            lo = (both - hi.astype(F32)).astype(BF16)
            row = lax.broadcasted_iota(jnp.int32, (EXTRA, HALF), 0)
            own[pl.ds(R, EXTRA), :] = jnp.where(
                row == 0, hi.astype(F32), jnp.where(row == 1, lo.astype(F32), 0.0)
            ).astype(BF16)
        a = send(own, w.at[xl, p, q], to_pp)
        b = send(own, w.at[xl, p, q], to_pm)
        kept = local(own, w.at[xl, p, q])
        yield
        arrived(a, b)
        a = send(w.at[xl, pm, q, low], w.at[xl, pm, q, low], to_pp)
        b = send(w.at[xl, pp, q, high], w.at[xl, pp, q, high], to_pm)
        yield
        kept.wait()
        arrived(a, b)
        a = send(w.at[xl, :, q], w.at[xl, :, q], to_qp)
        b = send(w.at[xl, :, q], w.at[xl, :, q], to_qm)
        yield
        arrived(a, b)
        a = send(w.at[xl, pl.ds(0, 2), qm], w.at[xl, pl.ds(0, 2), qm], to_qp)
        b = send(w.at[xl, pl.ds(2, 2), qp], w.at[xl, pl.ds(2, 2), qp], to_qm)
        yield
        arrived(a, b)
        a = send(w.at[xl, pl.ds(0, 2)], w.at[xl, pl.ds(0, 2)], to_xp)
        b = send(w.at[xl, pl.ds(2, 2)], w.at[xl, pl.ds(2, 2)], to_xm)
        yield
        arrived(a, b)
        yield

    def add(ref, index, *others):
        total = ref[index].astype(F32)
        for more in others:
            total = total + more.astype(F32)
        ref[index] = total.astype(BF16)

    def finish(own, l, store):
        copies = [send(own.at[c, xh], own.at[c, xh], to) for to in (to_rep, to_core, to_both)]
        yield
        arrived(*copies)
        for half in range(2):
            store(l, half, own[half, 0] + own[half, 1])
        yield

    def scatter_out(l):
        g, rows = s["gb", l], unit_rows(l)
        r1, r2, r3, r4, r5, r6 = (s["gb%d" % i, l] for i in range(1, 7))
        low, high = pl.ds(0, 64), pl.ds(64, rows - 64)
        a = send(g.at[1 - xl, pl.ds(0, 2)], r1.at[pl.ds(0, 2)], to_xp)
        b = send(g.at[1 - xl, pl.ds(2, 2)], r1.at[pl.ds(2, 2)], to_xm)
        yield
        arrived(a, b)

        def add_x(i, carry):
            for j in range(4):
                add(g, (xl, i, j), r1[i, j])
            return carry

        lax.fori_loop(0, 4, add_x, 0)
        a = send(g.at[xl, pl.ds(0, 2), q2], r2.at[pl.ds(0, 2)], to_qp)
        b = send(g.at[xl, pl.ds(2, 2), q2], r2.at[pl.ds(2, 2)], to_qm)
        yield
        arrived(a, b)
        for i in range(2):
            add(g, (xl, i, qp), r2[i])
            add(g, (xl, i + 2, qm), r2[i + 2])
        a = send(g.at[xl, :, qp], r3.at[0], to_qp)
        b = send(g.at[xl, :, qm], r3.at[1], to_qm)
        yield
        arrived(a, b)
        for i in range(4):
            add(g, (xl, i, q), r3[0, i], r3[1, i])
        a = send(g.at[xl, p2, q, low], r4.at[low], to_pp)
        b = send(g.at[xl, p2, q, high], r4.at[high], to_pm)
        yield
        arrived(a, b)
        add(g, (xl, pp, q, low), r4[low])
        add(g, (xl, pm, q, high), r4[high])
        a = send(g.at[xl, pp, q], r5.at[0], to_pp)
        b = send(g.at[xl, pm, q], r5.at[1], to_pm)
        yield
        arrived(a, b)
        r6[c, xh] = g[xl, p, q].astype(F32) + r5[0].astype(F32) + r5[1].astype(F32)
        yield from finish(r6, l, store_out)

    def scatter_in(l):
        g = s["ga", l]
        r1, r2, r3, r4, r5, r6 = (s["ga%d" % i, l] for i in range(1, 7))
        low, high = pl.ds(0, 64), pl.ds(64, 64)
        a = send(g.at[:, p2, pl.ds(0, 2)], r1.at[:, pl.ds(0, 2)], to_pp)
        b = send(g.at[:, p2, pl.ds(2, 2)], r1.at[:, pl.ds(2, 2)], to_pm)
        yield
        arrived(a, b)
        for x in range(2):
            for j in range(2):
                add(g, (x, pp, j), r1[x, j])
                add(g, (x, pm, j + 2), r1[x, j + 2])
        a = send(g.at[:, pp], r2.at[0], to_pp)
        b = send(g.at[:, pm], r2.at[1], to_pm)
        yield
        arrived(a, b)
        for x in range(2):
            for j in range(4):
                add(g, (x, p, j), r2[0, x, j], r2[1, x, j])
        a = send(g.at[:, p, q2, low], r3.at[:, low], to_qp)
        b = send(g.at[:, p, q2, high], r3.at[:, high], to_qm)
        yield
        arrived(a, b)
        for x in range(2):
            add(g, (x, p, qp, low), r3[x, low])
            add(g, (x, p, qm, high), r3[x, high])
        a = send(g.at[:, p, qp], r4.at[0], to_qp)
        b = send(g.at[:, p, qm], r4.at[1], to_qm)
        yield
        arrived(a, b)
        for x in range(2):
            add(g, (x, p, q), r4[0, x], r4[1, x])
        a = send(g.at[1 - xl, p, q], r5, to_pair)
        yield
        arrived(a)
        r6[c, xh] = g[xl, p, q].astype(F32) + r5[...].astype(F32)
        yield from finish(r6, l, store_in)

    def store_in(l, half, total):
        grad_in[l, pl.ds(half * HALF, HALF), :] = total.T

    def store_out(l, half, total):
        lanes = pl.ds(half * HALF, HALF)
        grad_out[l, :, lanes] = total[:R]
        if unit_rows(l) > R:
            vec = total[R : R + 8]
            row = lax.broadcasted_iota(jnp.int32, (8, HALF), 0)
            vec = jnp.sum(jnp.where(row == 0, vec, 0.0), axis=0, keepdims=True)
            grad_vec[0:1, lanes] = vec * pack[1:2, lanes]
            grad_vec[1:2, lanes] = vec * pack[0:1, lanes]

    def go(*jobs):
        for job in jobs:
            next(job, None)

    def lanes2(values):
        return jnp.concatenate([values, values], axis=1)

    def weights_out(l, i, j):
        w = s["wb", l]
        return jnp.concatenate([w[0, i, j, pl.ds(0, R)], w[1, i, j, pl.ds(0, R)]], axis=1)

    def squares(level):
        h, out = s["h", level], s["sq", level]
        out[...] = jnp.zeros_like(out)

        def step(i, carry):
            for r in range(0, ROWS, CHUNK):
                rows = pl.ds(r, CHUNK)
                total = out[rows, :]
                for j in range(4):
                    v = h[i, j, rows, :].astype(F32)
                    v = v * v
                    total = total + (v[:, :128] + v[:, 128:])
                out[rows, :] = total
            return carry

        lax.fori_loop(0, 4, step, 0)

    def down(l):
        h, w, out = s["h", l], s["wa", l], s["z", l]
        out[...] = jnp.zeros_like(out)

        def step(i, carry):
            lhs = jnp.concatenate([h[i, j] for j in range(4)], axis=1)
            out[...] += jnp.dot(lhs, w[i].reshape(4 * 2 * HALF, R), preferred_element_type=F32)
            return carry

        lax.fori_loop(0, 4, step, 0)

    def inverse(level):
        total = jnp.sum(s["sq", level][...] + s["sq_in", level][...], axis=1, keepdims=True)
        inv = lax.rsqrt(total * (1.0 / WIDTH) + EPS)
        s["rinv", level][...] = jnp.broadcast_to(inv, (ROWS, 128))

    def activate(l):
        v = (s["z", l][...] + s["z_in", l][...]) * s["rinv", l][...]
        s["z_in", l][...] = v
        active = v * jax.nn.sigmoid(v)
        s["act"][...] = active.astype(BF16)
        s["act_t", l][...] = active.T.astype(BF16)

    def up(l):
        h, out, sq = s["h", l], s["h", l + 1], s["sq", l + 1]
        last = l == LAYERS - 1
        sq[...] = jnp.zeros_like(sq)
        if last:
            s["q"][...] = jnp.zeros_like(s["q"])

        def step(i, carry):
            for j in range(4):
                w = weights_out(l, i, j)
                if last:
                    hg = s["hg"][i, j, 0:1, :]
                for r in range(0, ROWS, CHUNK):
                    rows = pl.ds(r, CHUNK)
                    v = jnp.dot(s["act"][rows, :], w, preferred_element_type=F32)
                    v = (h[i, j, rows, :].astype(F32) + v).astype(BF16)
                    out[i, j, rows, :] = v
                    v = v.astype(F32)
                    if last:
                        t = v * hg
                        s["q"][rows, :] += t[:, :128] + t[:, 128:]
                    v = v * v
                    sq[rows, :] += v[:, :128] + v[:, 128:]
            return carry

        lax.fori_loop(0, 4, step, 0)

    def gains():
        w = s["wb", LAYERS - 1]

        def step(i, carry):
            for j in range(4):
                for x in range(2):
                    rows = w[x, i, j, pl.ds(R, EXTRA)].astype(F32)
                    both = jnp.sum(rows, axis=0, keepdims=True)
                    s["hg"][i, j, :, pl.ds(x * HALF, HALF)] = jnp.broadcast_to(both, (8, HALF))
            return carry

        lax.fori_loop(0, 4, step, 0)

    def head():
        inv = s["rinv", LAYERS][...]
        dot_q = jnp.sum(s["q"][...] + s["q_in"][...], axis=1, keepdims=True)
        n_q = dot_q * inv
        seg_row = lax.broadcasted_iota(jnp.int32, (16, TOK), 0).astype(F32)
        onehots, rewards, counts = [], [], []
        for core in range(2):
            onehot = (s["packs"][core, 2:3, :] == seg_row).astype(F32)
            count = jnp.sum(onehot, axis=1, keepdims=True)
            total = jnp.dot(
                onehot,
                n_q[core * TOK : (core + 1) * TOK],
                precision=lax.Precision.HIGHEST,
                preferred_element_type=F32,
            )
            onehots.append(onehot)
            counts.append(count)
            rewards.append(total / count)
        place = lax.broadcasted_iota(jnp.int32, (8, 128), 0)
        lane = lax.broadcasted_iota(jnp.int32, (8, 128), 1)
        real = lane < 8
        for core in range(2):
            d_reward = []
            for k in range(2):
                order = s["packs"][core, 3 + k : 4 + k, 0:128]
                chosen = jnp.where(real & (order == place.astype(F32)), 1.0, 0.0)
                reward = rewards[core][8 * k : 8 * k + 8]
                placed = jnp.sum(chosen * reward, axis=0, keepdims=True)
                expo = jnp.exp(placed)
                suffix = jnp.sum(
                    jnp.where(real & (lane >= place), expo, 0.0), axis=1, keepdims=True
                )
                prefix = jnp.sum(
                    jnp.where(place <= lane, 1.0 / suffix, 0.0), axis=0, keepdims=True
                )
                d_placed = -1.0 + expo * prefix
                d_reward.append(
                    jnp.sum(jnp.where(chosen > 0.0, d_placed, 0.0), axis=1, keepdims=True)
                )
            scaled = jnp.concatenate(d_reward, axis=0) / counts[core]
            coef = lax.dot_general(
                onehots[core],
                jnp.broadcast_to(scaled, (16, 128)),
                (((0,), (0,)), ((), ())),
                precision=lax.Precision.HIGHEST,
                preferred_element_type=F32,
            )
            rows = pl.ds(core * TOK, TOK)
            inv_c = inv[core * TOK : (core + 1) * TOK]
            first = coef * inv_c
            s["coef"][rows, :] = first
            s["tok"][rows, :] = (
                first * inv_c * inv_c * dot_q[core * TOK : (core + 1) * TOK] * (1.0 / WIDTH)
            )
        vec = s["coef"][...].T[:8]
        hi = vec.astype(BF16)
        lo = (vec - hi.astype(F32)).astype(BF16)
        s["vec"][...] = jnp.concatenate([hi.astype(F32), lo.astype(F32)], axis=0).astype(BF16)

    def top():
        h, g = s["h", LAYERS], s["gb", LAYERS - 1]

        def step(i, carry):
            row = lax.broadcasted_iota(jnp.int32, (EXTRA, 256), 0)
            for j in range(4):
                vec = jnp.dot(s["vec"][...], h[i, j], preferred_element_type=F32)
                vec = jnp.where(row == 0, vec[:8][0:1] + vec[8:][0:1], 0.0).astype(BF16)
                g[0, i, j, pl.ds(R, EXTRA)] = vec[:, :HALF]
                g[1, i, j, pl.ds(R, EXTRA)] = vec[:, HALF:]
                hg = s["hg"][i, j, 0:1, :]
                for r in range(0, ROWS, CHUNK):
                    rows = pl.ds(r, CHUNK)
                    v = h[i, j, rows, :].astype(F32)
                    v = lanes2(s["coef"][rows, :]) * hg - v * lanes2(s["tok"][rows, :])
                    h[i, j, rows, :] = v.astype(BF16)
            return carry

        lax.fori_loop(0, 4, step, 0)

    def back_up(l):
        g, out = s["h", LAYERS], s["da", l]
        out[...] = jnp.zeros_like(out)

        def step(i, carry):
            lhs = jnp.concatenate([g[i, j] for j in range(4)], axis=1)
            rhs = jnp.concatenate([weights_out(l, i, j) for j in range(4)], axis=1)
            out[...] += lax.dot_general(lhs, rhs, NT, preferred_element_type=F32)
            return carry

        lax.fori_loop(0, 4, step, 0)

    def partial(lhs, wide, out):
        def step(i, carry):
            for j in range(4):
                v = jnp.dot(lhs[...], wide[i, j], preferred_element_type=F32).astype(BF16)
                out[0, i, j, pl.ds(0, R)] = v[:, :HALF]
                out[1, i, j, pl.ds(0, R)] = v[:, HALF:]
            return carry

        lax.fori_loop(0, 4, step, 0)

    def inner(l):
        v = s["z_in", l][...]
        inv = s["rinv", l][...]
        sigm = jax.nn.sigmoid(v)
        dz = (s["da", l][...] + s["da_in", l][...]) * sigm * (1.0 + v * (1.0 - sigm))
        mean = jnp.sum(dz * v, axis=1, keepdims=True) * (1.0 / WIDTH)
        s["tok"][...] = inv * inv * mean
        dz = dz * inv
        s["dzr"][...] = dz.astype(BF16)
        s["dzr_t"][...] = dz.T.astype(BF16)

    def back_down(l):
        g, h, w = s["h", LAYERS], s["h", l], s["wa", l]

        def step(i, carry):
            for j in range(4):
                rhs = w[i, j].reshape(2 * HALF, R)
                for r in range(0, ROWS, CHUNK):
                    rows = pl.ds(r, CHUNK)
                    du = lax.dot_general(s["dzr"][rows, :], rhs, NT, preferred_element_type=F32)
                    v = h[i, j, rows, :].astype(F32) * lanes2(s["tok"][rows, :])
                    g[i, j, rows, :] = (g[i, j, rows, :].astype(F32) + (du - v)).astype(BF16)
            return carry

        lax.fori_loop(0, 4, step, 0)

    in0, in1, in2 = (gather_in(l) for l in range(LAYERS))
    out0, out1, out2 = (gather_out(l) for l in range(LAYERS))
    go(in0, out0, in1, out1, in2, out2)

    core_send, core_recv = s["send"].at[N_SEMS - 1], s["recv"].at[N_SEMS - 1]

    def core_copy(src, dst):
        return pltpu.make_async_remote_copy(
            src_ref=src,
            dst_ref=dst,
            send_sem=core_send,
            recv_sem=core_recv,
            device_id=to_core,
            device_id_type=MESH,
        )

    def swap_hidden(i, carry):
        yy, zz = i // 4, i % 4
        for xx in range(2):
            col = pl.multiple_of(yy * 2048 + xx * 1024 + zz * 256 + other * HALF, HALF)
            core_copy(
                hidden.at[:, pl.ds(col, HALF)],
                s["h", 0].at[yy * c + zz * other, zz * c + yy * other, my_rows, pl.ds(xx * HALF, HALF)],
            ).start()
        return carry

    lax.fori_loop(0, 16, swap_hidden, 0)
    packs = send(pack, s["packs"].at[c], to_core)
    s["packs"][c] = pack[...]

    go(in0, out0, in1, out1)
    go(in0, out0, in1, out1)
    go(in0, out0, in2, out2)
    block = s["h", 0].at[:, :, my_rows]
    pltpu.make_async_copy(block, block, hidden_sem).wait()
    swapped = core_copy(block, s["h", 0].at[:, :, their_rows])
    swapped.wait_recv()
    swapped.wait_send()
    squares(0)
    sq = send(s["sq", 0], s["sq_in", 0], to_core)
    go(in0, out0, in1, out1, in2, out2)
    arrived(sq)
    inverse(0)
    go(in0)
    down(0)
    zc = send(s["z", 0], s["z_in", 0], to_core)
    go(out0, in1, out1, in2, out2)
    arrived(zc)
    activate(0)
    up(0)
    sq = send(s["sq", 1], s["sq_in", 1], to_core)
    go(in1)
    down(1)
    zc = send(s["z", 1], s["z_in", 1], to_core)
    go(out1, in2, out2)
    arrived(sq)
    inverse(1)
    arrived(zc)
    activate(1)
    up(1)
    sq = send(s["sq", 2], s["sq_in", 2], to_core)
    go(in2)
    down(2)
    zc = send(s["z", 2], s["z_in", 2], to_core)
    go(out2)
    gains()
    arrived(sq)
    inverse(2)
    arrived(zc)
    activate(2)
    up(2)
    sq = send(s["sq", 3], s["sq_in", 3], to_core)
    qc = send(s["q"], s["q_in"], to_core)
    arrived(packs, sq)
    inverse(3)
    arrived(qc)
    head()
    top()

    back_up(2)
    dc = send(s["da", 2], s["da_in", 2], to_core)
    partial(s["act_t", 2], s["h", LAYERS], s["gb", 2])
    out2 = scatter_out(2)
    go(out2)
    arrived(dc)
    inner(2)
    partial(s["dzr_t"], s["h", 2], s["ga", 2])
    in2 = scatter_in(2)
    go(in2)
    back_down(2)
    go(out2, in2)
    back_up(1)
    dc = send(s["da", 1], s["da_in", 1], to_core)
    go(out2)
    partial(s["act_t", 1], s["h", LAYERS], s["gb", 1])
    out1 = scatter_out(1)
    go(out1)
    go(out2, in2)
    arrived(dc)
    inner(1)
    partial(s["dzr_t"], s["h", 1], s["ga", 1])
    in1 = scatter_in(1)
    go(in1)
    go(out2, in2)
    back_down(1)
    go(out1, in1)
    back_up(0)
    dc = send(s["da", 0], s["da_in", 0], to_core)
    go(out2, in2, out1)
    partial(s["act_t", 0], s["h", LAYERS], s["gb", 0])
    out0 = scatter_out(0)
    go(out0)
    go(out2, in2)
    go(out1, in1)
    arrived(dc)
    inner(0)
    partial(s["dzr_t"], s["h", 0], s["ga", 0])
    in0 = scatter_in(0)
    go(in0)
    for _ in range(7):
        go(out2, in2, out1, in1, out0, in0)
    for copy in started:
        copy.wait_send()


def body(hidden, seg_ids, ranks, adapter_in, adapter_out, score_head, final_gain):
    pack = jnp.concatenate(
        [
            score_head.astype(F32)[None],
            final_gain.astype(F32)[None],
            seg_ids.astype(F32),
            jnp.pad(ranks[0].astype(F32), ((0, 0), (0, 248))),
            jnp.zeros((3, 256), F32),
        ],
        axis=0,
    )
    vmem = pl.BlockSpec(memory_space=pltpu.VMEM)
    hbm = pl.BlockSpec(memory_space=pl.ANY)
    grad_in, grad_out, grad_vec = pl.pallas_call(
        kernel,
        out_shape=(
            jax.ShapeDtypeStruct((LAYERS, 2 * HALF, R), F32),
            jax.ShapeDtypeStruct((LAYERS, R, 2 * HALF), F32),
            jax.ShapeDtypeStruct((8, 2 * HALF), F32),
        ),
        in_specs=[hbm, hbm, hbm, vmem],
        out_specs=(vmem, vmem, vmem),
        scratch_shapes=list(scratch().values()),
        compiler_params=pltpu.CompilerParams(
            collective_id=0, has_side_effects=True, vmem_limit_bytes=60 * 1024 * 1024
        ),
        name="adapters",
    )(hidden, adapter_in, adapter_out, pack)
    return grad_in, grad_out, grad_vec[0], grad_vec[1]


def solution(mesh):
    placed = (
        P(("rep", "shard"), None),
        P(("rep", "shard"), None),
        P(("rep", "shard"), None, None),
        P(None, "shard", None),
        P(None, None, "shard"),
        P("shard"),
        P("shard"),
    )
    return jax.shard_map(
        body,
        mesh=mesh,
        in_specs=placed,
        out_specs=(P(None, "shard", None), P(None, None, "shard"), P("shard"), P("shard")),
        check_vma=False,
    )
```

time: 2070 us -> 139 us (0.07)
  waiting for transfers between devices: 1770 us -> 0 us
  blocking collectives: 163 us -> 0 us
  Pallas kernels: 0 us -> 130 us
  matrix products: 70.2 us -> 0 us
  other arithmetic: 24.7 us -> 2.68 us
    reduce_scatter x6 -> x0, waiting for transfers between devices: 912 us -> none  [the longest x3 483 us: body(): lax.psum_scatter(grad_b.astype(jnp.bfloat16), 'shard', scatter_dimension=...]
    all_gather x6 -> x0, waiting for transfers between devices: 663 us -> none  [the longest x2 286 us: body(): lax.all_gather(adapter_in[layer], 'shard', axis=0, tiled=True)]
    unnamed x15 -> x0, waiting for transfers between devices: 162 us -> none
    all_gather x2 -> x0, blocking collectives: 132 us -> none  [the longest x1 69.8 us: body(): lax.all_gather(score_head, 'shard', axis=0, tiled=True)]
    pallas_call x0 -> x1, Pallas kernels: none -> 130 us  [body(): pl.pallas_call(kernel, out_shape=(jax.ShapeDtypeStruct((LAYERS, 2 * HALF,...]
    dot_general x20 -> x0, matrix products: 70.2 us -> none  [the longest x3 17.4 us: layer_forward(): outer = jnp.dot(active, w_out, preferred_element_type=jnp.float32)]
    psum x1 -> x0, waiting for transfers between devices: 34.7 us -> none  [body(): sum_a, sum_b, sum_x = lax.psum((stack_a, stack_b, red_x), 'rep')]
    psum x1 -> x0, blocking collectives: 31.1 us -> none  [body(): sum_a, sum_b, sum_x = lax.psum((stack_a, stack_b, red_x), 'rep')]
  transfers between devices with their start and end apart: 14 -> 0, of which waited for: 13 -> 0; matrix products, arithmetic and copies ran while one was open for 4% -> 0% of each run, Pallas kernels for 0% -> 0%
where the time goes in v1:
time: 139 us
  Pallas kernels  130 us (94%)
  local copies, waits for them, and re-layouts  5.5 us (4%)
  other arithmetic  2.68 us (2%)
    pallas_call x1, Pallas kernels, body(): pl.pallas_call(kernel, out_shape=(jax.ShapeDtypeStruct((LAYERS, 2 * HALF,...  130 us
    unnamed x2, local copies, waits for them, and re-layouts  3.53 us

profile of v1, /device:TPU:1, one launch (start us, length us, event | category | flops | bytes accessed | tf_op | source)
XLA Modules:
  0.0 139.0 jit_solution(8635229589992655701)
XLA Ops:
  0.6 0.7 convert_bitcast_fusion
  1.3 0.7 broadcast_in_dim.20
  2.0 0.7 broadcast_in_dim.21
  2.6 0.7 convert_element_type.13
  3.3 0.6 concatenate.3.pack
  3.9 130.2 %adapters.1 = (f32[3,256,128]{2,1,0:T(8,128)}, f32[3,128,256]{2,1,0:T(8,128)}, f32[8,256]{1,0:T(8,128)}) custom-call(bf16[256,8192]{1,0:T(8,128)(2,1)} %hidden.1, bf16[3,256,128]{2,1,0:T(8,128)(2,1)} %w_in.1, bf16[3,128,256]{2,1,0:T(8,128)(2,1)} %w_out.1, f32[8,256]{1,0:T(8,128)} %concatenate.3.pack), custom_call_target="tpu_custom_call" | custom-call | tf_op jit(solution)/shard_map/adapters/pallas_call | solution.py:683
  134.1 1.3 fusion
  135.5 1.8 %copy.13 = f32[3,256,128]{2,1,0:T(8,128)} copy(f32[3,256,128]{2,1,0:T(8,128)} %get-tuple-element.16) | data formatting | bytes 786432
  137.2 1.8 %copy.14 = f32[3,128,256]{2,1,0:T(8,128)} copy(f32[3,128,256]{2,1,0:T(8,128)} %get-tuple-element.17) | data formatting | bytes 786432
  (2 shorter events, 0.0 us)

commit v2 on v1

--- a/solution.py
+++ b/solution.py
@@ -16,7 +16,7 @@
 R = 128
 HALF = 128
 EXTRA = 16
-N_SEMS = 192
+N_SEMS = 240
 NT = (((1,), (1,)), ((), ()))
 CHUNK = 256
 
@@ -45,17 +45,14 @@
         shapes["ga", layer] = pltpu.VMEM((2, 4, 4, R, HALF), BF16)
         shapes["ga1", layer] = pltpu.VMEM((2, 4, R, HALF), BF16)
         shapes["ga2", layer] = pltpu.VMEM((2, 2, 4, R, HALF), BF16)
-        shapes["ga3", layer] = pltpu.VMEM((2, R, HALF), BF16)
-        shapes["ga4", layer] = pltpu.VMEM((2, 2, R, HALF), BF16)
-        shapes["ga5", layer] = pltpu.VMEM((R, HALF), BF16)
-        shapes["ga6", layer] = pltpu.VMEM((2, 2, R, HALF), F32)
+        shapes["ga3", layer] = pltpu.VMEM((2, 4, R, HALF), BF16)
+        shapes["ga4", layer] = pltpu.VMEM((2, 2, R, HALF), F32)
         shapes["gb", layer] = pltpu.VMEM((2, 4, 4, rows, HALF), BF16)
         shapes["gb1", layer] = pltpu.VMEM((4, 4, rows, HALF), BF16)
         shapes["gb2", layer] = pltpu.VMEM((4, rows, HALF), BF16)
         shapes["gb3", layer] = pltpu.VMEM((2, 4, rows, HALF), BF16)
-        shapes["gb4", layer] = pltpu.VMEM((rows, HALF), BF16)
-        shapes["gb5", layer] = pltpu.VMEM((2, rows, HALF), BF16)
-        shapes["gb6", layer] = pltpu.VMEM((2, 2, rows, HALF), F32)
+        shapes["gb4", layer] = pltpu.VMEM((3, rows, HALF), BF16)
+        shapes["gb5", layer] = pltpu.VMEM((2, 2, rows, HALF), F32)
     shapes["act"] = pltpu.VMEM((ROWS, R), BF16)
     shapes["dzr"] = pltpu.VMEM((ROWS, R), BF16)
     shapes["dzr_t"] = pltpu.VMEM((R, ROWS), BF16)
@@ -72,30 +69,34 @@
     return shapes
 
 
-def kernel(hidden, w_in, w_out, pack, grad_in, grad_out, grad_vec, *refs):
+def kernel(
+    hidden, seg_ids, ranks, w_in, w_out, score_head, final_gain,
+    grad_in, grad_out, grad_head, grad_gain, *refs
+):
     s = dict(zip(scratch(), refs))
     rep, shard = lax.axis_index("rep"), lax.axis_index("shard")
     xh, c = rep // 2, rep % 2
     y, xl, z = shard // 8, (shard // 4) % 2, shard % 4
     other = 1 - c
+    low, high = pl.ds(0, 2), pl.ds(2, 2)
     p, q = y * other + z * c, z * other + y * c
     pp, p2, pm = (p + 1) % 4, (p + 2) % 4, (p + 3) % 4
     qp, q2, qm = (q + 1) % 4, (q + 2) % 4, (q + 3) % 4
 
-    def at(y_by, z_by):
-        return (rep, (y + y_by) % 4 * 8 + xl * 4 + (z + z_by) % 4)
-
-    def along_x(by):
-        x = (xh * 2 + xl + by) % 4
-        return (x // 2 * 2 + c, y * 8 + x % 2 * 4 + z)
-
-    to_pp, to_pm = at(other, c), at(3 * other, 3 * c)
-    to_qp, to_qm = at(c, other), at(3 * c, 3 * other)
-    to_xp, to_xm = along_x(1), along_x(3)
-    to_pair = (rep, y * 8 + (1 - xl) * 4 + z)
+    def device(x_by, p_by, q_by):
+        x = (xh * 2 + xl + x_by) % 4
+        y_to = (y + p_by * other + q_by * c) % 4
+        z_to = (z + q_by * other + p_by * c) % 4
+        return (x // 2 * 2 + c, y_to * 8 + x % 2 * 4 + z_to)
+
+    to_p = [device(0, by, 0) for by in range(1, 4)]
+    to_q = [device(0, 0, by) for by in range(1, 4)]
+    to_xp = [device(1, 0, by) for by in range(4)]
+    to_xm = [device(3, 0, by) for by in range(4)]
     to_core = (xh * 2 + other, shard)
     to_rep = ((1 - xh) * 2 + c, shard)
     to_both = ((1 - xh) * 2 + other, shard)
+    to_x = to_xp[:2] + to_xm[2:]
 
     used = [0, 0]
     started = []
@@ -135,8 +136,14 @@
         local(w_out.at[l, :, mine], s["own", l].at[pl.ds(0, R)]) for l in range(LAYERS)
     ]
 
+    def head_row():
+        return score_head[...].astype(F32).reshape(1, 2 * HALF)
+
+    def gain_row():
+        return final_gain[...].astype(F32).reshape(1, 2 * HALF)
+
     barrier = pltpu.get_barrier_semaphore()
-    partners = (to_pp, to_pm, to_qp, to_qm, to_xp, to_xm, to_core, to_rep, to_both)
+    partners = (*to_p, *to_q, *to_xp, *to_xm, to_core, to_rep, to_both)
     for partner in partners:
         pl.semaphore_signal(barrier, inc=1, device_id=partner, device_id_type=MESH)
 
@@ -157,36 +164,32 @@
     pl.semaphore_wait(barrier, len(partners))
 
     def gather_in(l):
-        w = s["wa", l]
-        a = send(w_in.at[l, mine], w.at[p, q, xl], to_pair)
+        w, src = s["wa", l], w_in.at[l, mine]
+        copies = [send(src, w.at[p, q, xl], to) for to in (*to_q, *to_x)]
         yield
         local_in[l].wait()
-        arrived(a)
-        a = send(w.at[p, q], w.at[p, q], to_qp)
-        b = send(w.at[p, q], w.at[p, q], to_qm)
+        arrived(*copies)
+        a = send(w.at[p, low], w.at[p, low], to_p[0])
+        b = send(w.at[p, high], w.at[p, high], to_p[2])
+        copies = [
+            send(w.at[p, high], w.at[p, high], to_p[0]),
+            send(w.at[p, low], w.at[p, low], to_p[2]),
+        ]
         yield
         arrived(a, b)
-        a = send(w.at[p, qm, 0], w.at[p, qm, 0], to_qp)
-        b = send(w.at[p, qp, 1], w.at[p, qp, 1], to_qm)
-        yield
-        arrived(a, b)
-        a = send(w.at[p], w.at[p], to_pp)
-        b = send(w.at[p], w.at[p], to_pm)
-        yield
-        arrived(a, b)
-        a = send(w.at[pm, pl.ds(0, 2)], w.at[pm, pl.ds(0, 2)], to_pp)
-        b = send(w.at[pp, pl.ds(2, 2)], w.at[pp, pl.ds(2, 2)], to_pm)
-        yield
-        arrived(a, b)
+        copies += [
+            send(w.at[pm, low], w.at[pm, low], to_p[0]),
+            send(w.at[pp, high], w.at[pp, high], to_p[2]),
+        ]
+        yield
+        arrived(*copies)
         yield
 
     def gather_out(l):
         w, own, rows = s["wb", l], s["own", l], unit_rows(l)
-        low, high = pl.ds(0, 64), pl.ds(64, rows - 64)
         local_out[l].wait()
         if rows > R:
-            head, gain = pack[0:1, :], pack[1:2, :]
-            both = head * gain
+            both = head_row() * gain_row()
             both = both[:, :HALF] * (1 - c).astype(F32) + both[:, HALF:] * c.astype(F32)
             hi = both.astype(BF16)
             lo = (both - hi.astype(F32)).astype(BF16)
@@ -194,35 +197,48 @@
             own[pl.ds(R, EXTRA), :] = jnp.where(
                 row == 0, hi.astype(F32), jnp.where(row == 1, lo.astype(F32), 0.0)
             ).astype(BF16)
-        a = send(own, w.at[xl, p, q], to_pp)
-        b = send(own, w.at[xl, p, q], to_pm)
+        copies = [send(own, w.at[xl, p, q], to) for to in to_p]
         kept = local(own, w.at[xl, p, q])
         yield
+        kept.wait()
+        arrived(*copies)
+        a = send(w.at[xl, low, q], w.at[xl, low, q], to_q[0])
+        b = send(w.at[xl, high, q], w.at[xl, high, q], to_q[2])
+        copies = [
+            send(w.at[xl, high, q], w.at[xl, high, q], to_q[0]),
+            send(w.at[xl, low, q], w.at[xl, low, q], to_q[2]),
+        ]
+        across = [
+            send(w.at[xl, low, q], w.at[xl, low, q], to_xp[0]),
+            send(w.at[xl, high, q], w.at[xl, high, q], to_xm[0]),
+        ]
+        yield
         arrived(a, b)
-        a = send(w.at[xl, pm, q, low], w.at[xl, pm, q, low], to_pp)
-        b = send(w.at[xl, pp, q, high], w.at[xl, pp, q, high], to_pm)
-        yield
-        kept.wait()
-        arrived(a, b)
-        a = send(w.at[xl, :, q], w.at[xl, :, q], to_qp)
-        b = send(w.at[xl, :, q], w.at[xl, :, q], to_qm)
-        yield
-        arrived(a, b)
-        a = send(w.at[xl, pl.ds(0, 2), qm], w.at[xl, pl.ds(0, 2), qm], to_qp)
-        b = send(w.at[xl, pl.ds(2, 2), qp], w.at[xl, pl.ds(2, 2), qp], to_qm)
-        yield
-        arrived(a, b)
-        a = send(w.at[xl, pl.ds(0, 2)], w.at[xl, pl.ds(0, 2)], to_xp)
-        b = send(w.at[xl, pl.ds(2, 2)], w.at[xl, pl.ds(2, 2)], to_xm)
-        yield
-        arrived(a, b)
-        yield
-
-    def add(ref, index, *others):
-        total = ref[index].astype(F32)
-        for more in others:
-            total = total + more.astype(F32)
-        ref[index] = total.astype(BF16)
+        copies += [
+            send(w.at[xl, low, qm], w.at[xl, low, qm], to_q[0]),
+            send(w.at[xl, high, qp], w.at[xl, high, qp], to_q[2]),
+        ]
+        across += [
+            send(w.at[xl, low, qm], w.at[xl, low, qm], to_xp[0]),
+            send(w.at[xl, high, qp], w.at[xl, high, qp], to_xm[0]),
+        ]
+        yield
+        arrived(*copies)
+        across += [
+            send(w.at[xl, low, qp], w.at[xl, low, qp], to_xp[0]),
+            send(w.at[xl, high, qm], w.at[xl, high, qm], to_xm[0]),
+            send(w.at[xl, low, q2], w.at[xl, low, q2], to_xp[0]),
+            send(w.at[xl, high, q2], w.at[xl, high, q2], to_xm[0]),
+        ]
+        yield
+        arrived(*across)
+        yield
+
+    def total(*parts):
+        value = parts[0].astype(F32)
+        for part in parts[1:]:
+            value = value + part.astype(F32)
+        return value
 
     def finish(own, l, store):
         copies = [send(own.at[c, xh], own.at[c, xh], to) for to in (to_rep, to_core, to_both)]
@@ -233,83 +249,81 @@
         yield
 
     def scatter_out(l):
-        g, rows = s["gb", l], unit_rows(l)
-        r1, r2, r3, r4, r5, r6 = (s["gb%d" % i, l] for i in range(1, 7))
-        low, high = pl.ds(0, 64), pl.ds(64, rows - 64)
-        a = send(g.at[1 - xl, pl.ds(0, 2)], r1.at[pl.ds(0, 2)], to_xp)
-        b = send(g.at[1 - xl, pl.ds(2, 2)], r1.at[pl.ds(2, 2)], to_xm)
-        yield
-        arrived(a, b)
-
-        def add_x(i, carry):
-            for j in range(4):
-                add(g, (xl, i, j), r1[i, j])
-            return carry
-
-        lax.fori_loop(0, 4, add_x, 0)
-        a = send(g.at[xl, pl.ds(0, 2), q2], r2.at[pl.ds(0, 2)], to_qp)
-        b = send(g.at[xl, pl.ds(2, 2), q2], r2.at[pl.ds(2, 2)], to_qm)
-        yield
+        g = s["gb", l]
+        r1, r2, r3, r4, r5 = (s["gb%d" % i, l] for i in range(1, 6))
+        across = []
+        for j in (q2, qp, qm, q):
+            across += [
+                send(g.at[1 - xl, low, j], r1.at[low, j], to_xp[0]),
+                send(g.at[1 - xl, high, j], r1.at[high, j], to_xm[0]),
+            ]
+        yield
+        arrived(*across[:2])
+        for i in range(4):
+            g[xl, i, q2] = total(g[xl, i, q2], r1[i, q2]).astype(BF16)
+        a = send(g.at[xl, low, q2], r2.at[low], to_q[0])
+        b = send(g.at[xl, high, q2], r2.at[high], to_q[2])
+        yield
+        arrived(*across[2:6])
+        for i in range(2):
+            g[xl, i + 2, qp] = total(g[xl, i + 2, qp], r1[i + 2, qp]).astype(BF16)
+            g[xl, i, qm] = total(g[xl, i, qm], r1[i, qm]).astype(BF16)
+        copies = [
+            send(g.at[xl, high, qp], r3.at[0, high], to_q[0]),
+            send(g.at[xl, low, qm], r3.at[1, low], to_q[2]),
+        ]
         arrived(a, b)
         for i in range(2):
-            add(g, (xl, i, qp), r2[i])
-            add(g, (xl, i + 2, qm), r2[i + 2])
-        a = send(g.at[xl, :, qp], r3.at[0], to_qp)
-        b = send(g.at[xl, :, qm], r3.at[1], to_qm)
-        yield
-        arrived(a, b)
+            g[xl, i, qp] = total(g[xl, i, qp], r1[i, qp], r2[i]).astype(BF16)
+            g[xl, i + 2, qm] = total(g[xl, i + 2, qm], r1[i + 2, qm], r2[i + 2]).astype(BF16)
+        copies += [
+            send(g.at[xl, low, qp], r3.at[0, low], to_q[0]),
+            send(g.at[xl, high, qm], r3.at[1, high], to_q[2]),
+        ]
+        yield
+        arrived(*across[6:], *copies)
         for i in range(4):
-            add(g, (xl, i, q), r3[0, i], r3[1, i])
-        a = send(g.at[xl, p2, q, low], r4.at[low], to_pp)
-        b = send(g.at[xl, p2, q, high], r4.at[high], to_pm)
-        yield
-        arrived(a, b)
-        add(g, (xl, pp, q, low), r4[low])
-        add(g, (xl, pm, q, high), r4[high])
-        a = send(g.at[xl, pp, q], r5.at[0], to_pp)
-        b = send(g.at[xl, pm, q], r5.at[1], to_pm)
-        yield
-        arrived(a, b)
-        r6[c, xh] = g[xl, p, q].astype(F32) + r5[0].astype(F32) + r5[1].astype(F32)
-        yield from finish(r6, l, store_out)
+            g[xl, i, q] = total(g[xl, i, q], r1[i, q], r3[0, i], r3[1, i]).astype(BF16)
+        copies = [send(g.at[xl, (p + 1 + k) % 4, q], r4.at[k], to_p[k]) for k in range(3)]
+        yield
+        arrived(*copies)
+        r5[c, xh] = total(g[xl, p, q], r4[0], r4[1], r4[2])
+        yield from finish(r5, l, store_out)
 
     def scatter_in(l):
         g = s["ga", l]
-        r1, r2, r3, r4, r5, r6 = (s["ga%d" % i, l] for i in range(1, 7))
-        low, high = pl.ds(0, 64), pl.ds(64, 64)
-        a = send(g.at[:, p2, pl.ds(0, 2)], r1.at[:, pl.ds(0, 2)], to_pp)
-        b = send(g.at[:, p2, pl.ds(2, 2)], r1.at[:, pl.ds(2, 2)], to_pm)
+        r1, r2, r3, r4 = (s["ga%d" % i, l] for i in range(1, 5))
+        a = send(g.at[:, p2, low], r1.at[:, low], to_p[0])
+        b = send(g.at[:, p2, high], r1.at[:, high], to_p[2])
+        copies = [
+            send(g.at[:, pp, high], r2.at[0, :, high], to_p[0]),
+            send(g.at[:, pm, low], r2.at[1, :, low], to_p[2]),
+        ]
         yield
         arrived(a, b)
         for x in range(2):
             for j in range(2):
-                add(g, (x, pp, j), r1[x, j])
-                add(g, (x, pm, j + 2), r1[x, j + 2])
-        a = send(g.at[:, pp], r2.at[0], to_pp)
-        b = send(g.at[:, pm], r2.at[1], to_pm)
-        yield
-        arrived(a, b)
+                g[x, pp, j] = total(g[x, pp, j], r1[x, j]).astype(BF16)
+                g[x, pm, j + 2] = total(g[x, pm, j + 2], r1[x, j + 2]).astype(BF16)
+        copies += [
+            send(g.at[:, pp, low], r2.at[0, :, low], to_p[0]),
+            send(g.at[:, pm, high], r2.at[1, :, high], to_p[2]),
+        ]
+        yield
+        arrived(*copies)
         for x in range(2):
             for j in range(4):
-                add(g, (x, p, j), r2[0, x, j], r2[1, x, j])
-        a = send(g.at[:, p, q2, low], r3.at[:, low], to_qp)
-        b = send(g.at[:, p, q2, high], r3.at[:, high], to_qm)
-        yield
-        arrived(a, b)
-        for x in range(2):
-            add(g, (x, p, qp, low), r3[x, low])
-            add(g, (x, p, qm, high), r3[x, high])
-        a = send(g.at[:, p, qp], r4.at[0], to_qp)
-        b = send(g.at[:, p, qm], r4.at[1], to_qm)
-        yield
-        arrived(a, b)
-        for x in range(2):
-            add(g, (x, p, q), r4[0, x], r4[1, x])
-        a = send(g.at[1 - xl, p, q], r5, to_pair)
-        yield
-        arrived(a)
-        r6[c, xh] = g[xl, p, q].astype(F32) + r5[...].astype(F32)
-        yield from finish(r6, l, store_in)
+                g[x, p, j] = total(g[x, p, j], r2[0, x, j], r2[1, x, j]).astype(BF16)
+        copies = [send(g.at[xl, p, (q + 1 + k) % 4], r3.at[0, k + 1], to_q[k]) for k in range(3)]
+        copies += [send(g.at[1 - xl, p, (q + k) % 4], r3.at[1, k], to_x[k]) for k in range(4)]
+        yield
+        arrived(*copies)
+        r4[c, xh] = total(
+            g[xl, p, q], *[r3[0, k] for k in range(1, 4)], *[r3[1, k] for k in range(4)]
+        )
+        yield from finish(r4, l, store_in)
+
+    vecs = []
 
     def store_in(l, half, total):
         grad_in[l, pl.ds(half * HALF, HALF), :] = total.T
@@ -321,8 +335,11 @@
             vec = total[R : R + 8]
             row = lax.broadcasted_iota(jnp.int32, (8, HALF), 0)
             vec = jnp.sum(jnp.where(row == 0, vec, 0.0), axis=0, keepdims=True)
-            grad_vec[0:1, lanes] = vec * pack[1:2, lanes]
-            grad_vec[1:2, lanes] = vec * pack[0:1, lanes]
+            vecs.append(vec)
+            if half == 1:
+                vec = jnp.concatenate(vecs, axis=1)
+                grad_head[...] = (vec * gain_row()).reshape(2 * HALF)
+                grad_gain[...] = (vec * head_row()).reshape(2 * HALF)
 
     def go(*jobs):
         for job in jobs:
@@ -544,7 +561,7 @@
 
     in0, in1, in2 = (gather_in(l) for l in range(LAYERS))
     out0, out1, out2 = (gather_out(l) for l in range(LAYERS))
-    go(in0, out0, in1, out1, in2, out2)
+    go(in0, out0)
 
     core_send, core_recv = s["send"].at[N_SEMS - 1], s["recv"].at[N_SEMS - 1]
 
@@ -569,12 +586,12 @@
         return carry
 
     lax.fori_loop(0, 16, swap_hidden, 0)
-    packs = send(pack, s["packs"].at[c], to_core)
-    s["packs"][c] = pack[...]
-
-    go(in0, out0, in1, out1)
-    go(in0, out0, in1, out1)
-    go(in0, out0, in2, out2)
+    s["packs"][c, 2:3, :] = seg_ids[...].astype(F32)
+    s["packs"][c, 3:5, 0:8] = ranks[0].astype(F32)
+    packs = send(s["packs"].at[c], s["packs"].at[c], to_core)
+
+    go(in1, out1, in2, out2)
+    go(in0, out0, in1, out1, in2, out2)
     block = s["h", 0].at[:, :, my_rows]
     pltpu.make_async_copy(block, block, hidden_sem).wait()
     swapped = core_copy(block, s["h", 0].at[:, :, their_rows])
@@ -582,34 +599,35 @@
     swapped.wait_send()
     squares(0)
     sq = send(s["sq", 0], s["sq_in", 0], to_core)
-    go(in0, out0, in1, out1, in2, out2)
+    go(in0, out0, in1, out1)
     arrived(sq)
     inverse(0)
-    go(in0)
+    go(out0, in0)
     down(0)
     zc = send(s["z", 0], s["z_in", 0], to_core)
-    go(out0, in1, out1, in2, out2)
+    go(out1, in2, out2)
     arrived(zc)
     activate(0)
+    go(out0)
     up(0)
     sq = send(s["sq", 1], s["sq_in", 1], to_core)
-    go(in1)
+    go(in1, out2)
     down(1)
     zc = send(s["z", 1], s["z_in", 1], to_core)
-    go(out1, in2, out2)
     arrived(sq)
     inverse(1)
     arrived(zc)
     activate(1)
+    go(out1)
     up(1)
     sq = send(s["sq", 2], s["sq_in", 2], to_core)
     go(in2)
     down(2)
     zc = send(s["z", 2], s["z_in", 2], to_core)
+    arrived(sq)
+    inverse(2)
     go(out2)
     gains()
-    arrived(sq)
-    inverse(2)
     arrived(zc)
     activate(2)
     up(2)
@@ -632,70 +650,69 @@
     in2 = scatter_in(2)
     go(in2)
     back_down(2)
-    go(out2, in2)
+    go(out2)
     back_up(1)
     dc = send(s["da", 1], s["da_in", 1], to_core)
-    go(out2)
     partial(s["act_t", 1], s["h", LAYERS], s["gb", 1])
     out1 = scatter_out(1)
-    go(out1)
-    go(out2, in2)
+    go(out1, in2, out2)
     arrived(dc)
     inner(1)
     partial(s["dzr_t"], s["h", 1], s["ga", 1])
     in1 = scatter_in(1)
-    go(in1)
-    go(out2, in2)
+    go(in1, out1)
     back_down(1)
-    go(out1, in1)
+    go(in2, out2)
     back_up(0)
     dc = send(s["da", 0], s["da_in", 0], to_core)
-    go(out2, in2, out1)
     partial(s["act_t", 0], s["h", LAYERS], s["gb", 0])
     out0 = scatter_out(0)
-    go(out0)
-    go(out2, in2)
-    go(out1, in1)
+    go(out0, in1, out1)
     arrived(dc)
     inner(0)
     partial(s["dzr_t"], s["h", 0], s["ga", 0])
     in0 = scatter_in(0)
-    go(in0)
-    for _ in range(7):
-        go(out2, in2, out1, in1, out0, in0)
+    go(in0, out0, in2, out2, in1, out1)
+    go(in0, out0, in2, out2, in1, out1)
+    go(in0, out0, in1, out1)
+    go(in0, out0)
+    go(in0, out0)
     for copy in started:
         copy.wait_send()
 
 
+def deliver(*refs):
+    for i in range(4):
+        refs[i + 4][...] = refs[i][...]
+
+
 def body(hidden, seg_ids, ranks, adapter_in, adapter_out, score_head, final_gain):
-    pack = jnp.concatenate(
-        [
-            score_head.astype(F32)[None],
-            final_gain.astype(F32)[None],
-            seg_ids.astype(F32),
-            jnp.pad(ranks[0].astype(F32), ((0, 0), (0, 248))),
-            jnp.zeros((3, 256), F32),
-        ],
-        axis=0,
-    )
     vmem = pl.BlockSpec(memory_space=pltpu.VMEM)
     hbm = pl.BlockSpec(memory_space=pl.ANY)
-    grad_in, grad_out, grad_vec = pl.pallas_call(
+    shapes = (
+        jax.ShapeDtypeStruct((LAYERS, 2 * HALF, R), F32),
+        jax.ShapeDtypeStruct((LAYERS, R, 2 * HALF), F32),
+        jax.ShapeDtypeStruct((2 * HALF,), F32),
+        jax.ShapeDtypeStruct((2 * HALF,), F32),
+    )
+    grads = pl.pallas_call(
         kernel,
-        out_shape=(
-            jax.ShapeDtypeStruct((LAYERS, 2 * HALF, R), F32),
-            jax.ShapeDtypeStruct((LAYERS, R, 2 * HALF), F32),
-            jax.ShapeDtypeStruct((8, 2 * HALF), F32),
-        ),
-        in_specs=[hbm, hbm, hbm, vmem],
-        out_specs=(vmem, vmem, vmem),
+        out_shape=shapes,
+        in_specs=[hbm, vmem, vmem, hbm, hbm, vmem, vmem],
+        out_specs=(vmem,) * 4,
         scratch_shapes=list(scratch().values()),
         compiler_params=pltpu.CompilerParams(
             collective_id=0, has_side_effects=True, vmem_limit_bytes=60 * 1024 * 1024
         ),
         name="adapters",
-    )(hidden, adapter_in, adapter_out, pack)
-    return grad_in, grad_out, grad_vec[0], grad_vec[1]
+    )(hidden, seg_ids, ranks, adapter_in, adapter_out, score_head, final_gain)
+    return pl.pallas_call(
+        deliver,
+        out_shape=shapes,
+        in_specs=[vmem] * 4,
+        out_specs=(vmem,) * 4,
+        name="deliver",
+    )(*grads)
 
 
 def solution(mesh):

time: 139 us -> 116 us (0.83)
  Pallas kernels: 130 us -> 116 us
  local copies, waits for them, and re-layouts: 5.5 us -> 0 us
  other arithmetic: 2.68 us -> 0 us
    pallas_call x1 -> x2, Pallas kernels: 130 us -> 116 us  [the longest x1 114 us: body(): pl.pallas_call(kernel, out_shape=shapes, in_specs=[hbm, vmem, vmem, hbm,...]
    unnamed x2 -> x0, local copies, waits for them, and re-layouts: 3.53 us -> none
where the time goes in v2:
time: 116 us
  Pallas kernels  116 us (100%)
    pallas_call x1, Pallas kernels, body(): pl.pallas_call(kernel, out_shape=shapes, in_specs=[hbm, vmem, vmem, hbm,...  114 us

profile of v2, /device:TPU:1, one launch (start us, length us, event | category | flops | bytes accessed | tf_op | source)
XLA Modules:
  0.0 116.3 jit_solution(10403966043750738530)
XLA Ops:
  0.6 113.7 %adapters.1 = (f32[3,256,128]{2,1,0:T(8,128)}, f32[3,128,256]{2,1,0:T(8,128)}, f32[256]{0:T(256)}, f32[256]{0:T(256)}) custom-call(bf16[256,8192]{1,0:T(8,128)(2,1)} %hidden.1, s32[1,256]{1,0:T(1,128)} %seg_ids.1, s32[1,2,8]{2,1,0:T(2,128)} %ranks.1, bf16[3,256,128]{2,1,0:T(8,128)(2,1)} %w_in.1, bf16[3,128,256]{2,1,0:T(8,128)(2,1)} %w_out.1, ...), custom_call_target="tpu_custom_call" | custom-call | tf_op jit(solution)/shard_map/adapters/pallas_call | solution.py:698
  114.3 2.0 %deliver.1 = (f32[3,256,128]{2,1,0:T(8,128)}, f32[3,128,256]{2,1,0:T(8,128)}, f32[256]{0:T(256)}, f32[256]{0:T(256)}) custom-call(f32[3,256,128]{2,1,0:T(8,128)} %get-tuple-element.8.refs_0_, f32[3,128,256]{2,1,0:T(8,128)} %get-tuple-element.9.refs_1_, f32[256]{0:T(256)} %get-tuple-element.10.refs_2_, f32[256]{0:T(256)} %get-tuple-element.11.refs_3_), custom_call_target="tpu_custom_call" | custom-call | tf_op jit(solution)/shard_map/deliver/pallas_call | solution.py:709

commit v3 on v2

--- a/solution.py
+++ b/solution.py
@@ -20,10 +20,8 @@
 NT = (((1,), (1,)), ((), ()))
 CHUNK = 256
 
-
 def unit_rows(layer):
     return R + EXTRA if layer == LAYERS - 1 else R
-
 
 def scratch():
     shapes = {}
@@ -46,13 +44,15 @@
         shapes["ga1", layer] = pltpu.VMEM((2, 4, R, HALF), BF16)
         shapes["ga2", layer] = pltpu.VMEM((2, 2, 4, R, HALF), BF16)
         shapes["ga3", layer] = pltpu.VMEM((2, 4, R, HALF), BF16)
-        shapes["ga4", layer] = pltpu.VMEM((2, 2, R, HALF), F32)
+        shapes["ga4", layer] = pltpu.VMEM((2, R, HALF), BF16)
+        shapes["ga5", layer] = pltpu.VMEM((2, R, HALF), F32)
         shapes["gb", layer] = pltpu.VMEM((2, 4, 4, rows, HALF), BF16)
         shapes["gb1", layer] = pltpu.VMEM((4, 4, rows, HALF), BF16)
         shapes["gb2", layer] = pltpu.VMEM((4, rows, HALF), BF16)
         shapes["gb3", layer] = pltpu.VMEM((2, 4, rows, HALF), BF16)
         shapes["gb4", layer] = pltpu.VMEM((3, rows, HALF), BF16)
-        shapes["gb5", layer] = pltpu.VMEM((2, 2, rows, HALF), F32)
+        shapes["gb5", layer] = pltpu.VMEM((2, rows, HALF), BF16)
+        shapes["gb6", layer] = pltpu.VMEM((2, rows, HALF), F32)
     shapes["act"] = pltpu.VMEM((ROWS, R), BF16)
     shapes["dzr"] = pltpu.VMEM((ROWS, R), BF16)
     shapes["dzr_t"] = pltpu.VMEM((R, ROWS), BF16)
@@ -62,12 +62,19 @@
     shapes["coef"] = pltpu.VMEM((ROWS, 128), F32)
     shapes["vec"] = pltpu.VMEM((16, ROWS), BF16)
     shapes["hg"] = pltpu.VMEM((4, 4, 8, 2 * HALF), F32)
+    shapes["seg"] = pltpu.VMEM((1, TOK), jnp.int32)
+    shapes["ranks"] = pltpu.VMEM((1, 2, 8), jnp.int32)
+    shapes["score"] = pltpu.VMEM((2 * HALF,), BF16)
+    shapes["gain"] = pltpu.VMEM((2 * HALF,), BF16)
+    shapes["out_in"] = pltpu.VMEM((LAYERS, 2 * HALF, R), F32)
+    shapes["out_out"] = pltpu.VMEM((LAYERS, R, 2 * HALF), F32)
+    shapes["out_head"] = pltpu.VMEM((2 * HALF,), F32)
+    shapes["out_gain"] = pltpu.VMEM((2 * HALF,), F32)
     shapes["packs"] = pltpu.VMEM((2, 8, 256), F32)
     shapes["send"] = pltpu.SemaphoreType.DMA((N_SEMS,))
     shapes["recv"] = pltpu.SemaphoreType.DMA((N_SEMS,))
-    shapes["local"] = pltpu.SemaphoreType.DMA((16,))
+    shapes["local"] = pltpu.SemaphoreType.DMA((32,))
     return shapes
-
 
 def kernel(
     hidden, seg_ids, ranks, w_in, w_out, score_head, final_gain,
@@ -95,7 +102,6 @@
     to_xm = [device(3, 0, by) for by in range(4)]
     to_core = (xh * 2 + other, shard)
     to_rep = ((1 - xh) * 2 + c, shard)
-    to_both = ((1 - xh) * 2 + other, shard)
     to_x = to_xp[:2] + to_xm[2:]
 
     used = [0, 0]
@@ -129,25 +135,34 @@
     mine = pl.ds(pl.multiple_of(c * HALF, HALF), HALF)
     my_rows = pl.ds(pl.multiple_of(c * TOK, TOK), TOK)
     their_rows = pl.ds(pl.multiple_of(other * TOK, TOK), TOK)
+    def head_row():
+        return s["score"][...].astype(F32).reshape(1, 2 * HALF)
+
+    def gain_row():
+        return s["gain"][...].astype(F32).reshape(1, 2 * HALF)
+
+    barrier = pltpu.get_barrier_semaphore()
+    partners = (*to_p, *to_q, *to_xp, *to_xm, to_core, to_rep)
+    for partner in partners:
+        pl.semaphore_signal(barrier, inc=1, device_id=partner, device_id_type=MESH)
+
     local_in = [
         local(w_in.at[l, mine], s["wa", l].at[p, q, xl]) for l in range(LAYERS)
     ]
     local_out = [
         local(w_out.at[l, :, mine], s["own", l].at[pl.ds(0, R)]) for l in range(LAYERS)
     ]
-
-    def head_row():
-        return score_head[...].astype(F32).reshape(1, 2 * HALF)
-
-    def gain_row():
-        return final_gain[...].astype(F32).reshape(1, 2 * HALF)
-
-    barrier = pltpu.get_barrier_semaphore()
-    partners = (*to_p, *to_q, *to_xp, *to_xm, to_core, to_rep, to_both)
-    for partner in partners:
-        pl.semaphore_signal(barrier, inc=1, device_id=partner, device_id_type=MESH)
-
-    hidden_sem = s["local"].at[15]
+    local_small = [
+        local(src, s[name])
+        for src, name in (
+            (seg_ids, "seg"),
+            (ranks, "ranks"),
+            (score_head, "score"),
+            (final_gain, "gain"),
+        )
+    ]
+
+    hidden_sem = s["local"].at[31]
 
     def load_hidden(i, carry):
         yy, zz = i // 4, i % 4
@@ -240,19 +255,26 @@
             value = value + part.astype(F32)
         return value
 
-    def finish(own, l, store):
-        copies = [send(own.at[c, xh], own.at[c, xh], to) for to in (to_rep, to_core, to_both)]
-        yield
-        arrived(*copies)
+    def finish(own, whole, l, store):
+        copy = send(own.at[xh], own.at[xh], to_rep)
+        yield
+        arrived(copy)
+        whole[c] = total(own[0], own[1])
+        copy = send(whole.at[c], whole.at[c], to_core)
+        yield
+        arrived(copy)
         for half in range(2):
-            store(l, half, own[half, 0] + own[half, 1])
+            store(l, half, whole[half])
         yield
 
     def scatter_out(l):
         g = s["gb", l]
-        r1, r2, r3, r4, r5 = (s["gb%d" % i, l] for i in range(1, 6))
+        r1, r2, r3, r4, r5, r6 = (s["gb%d" % i, l] for i in range(1, 7))
         across = []
         for j in (q2, qp, qm, q):
+            if l == LAYERS - 1:
+                top(j)
+            partial(s["act_t", l], s["h", LAYERS], g, [(i, j) for i in range(4)])
             across += [
                 send(g.at[1 - xl, low, j], r1.at[low, j], to_xp[0]),
                 send(g.at[1 - xl, high, j], r1.at[high, j], to_xm[0]),
@@ -287,18 +309,22 @@
         copies = [send(g.at[xl, (p + 1 + k) % 4, q], r4.at[k], to_p[k]) for k in range(3)]
         yield
         arrived(*copies)
-        r5[c, xh] = total(g[xl, p, q], r4[0], r4[1], r4[2])
-        yield from finish(r5, l, store_out)
+        r5[xh] = total(g[xl, p, q], r4[0], r4[1], r4[2]).astype(BF16)
+        yield from finish(r5, r6, l, store_out)
 
     def scatter_in(l):
         g = s["ga", l]
-        r1, r2, r3, r4 = (s["ga%d" % i, l] for i in range(1, 5))
+        r1, r2, r3, r4, r5 = (s["ga%d" % i, l] for i in range(1, 6))
+        partial(s["dzr_t"], s["h", l], g, [(p2, j) for j in range(4)])
         a = send(g.at[:, p2, low], r1.at[:, low], to_p[0])
         b = send(g.at[:, p2, high], r1.at[:, high], to_p[2])
+        partial(s["dzr_t"], s["h", l], g, [(pp, j) for j in (2, 3)] + [(pm, j) for j in (0, 1)])
         copies = [
             send(g.at[:, pp, high], r2.at[0, :, high], to_p[0]),
             send(g.at[:, pm, low], r2.at[1, :, low], to_p[2]),
         ]
+        partial(s["dzr_t"], s["h", l], g, [(pp, j) for j in (0, 1)] + [(pm, j) for j in (2, 3)])
+        partial(s["dzr_t"], s["h", l], g, [(p, j) for j in range(4)])
         yield
         arrived(a, b)
         for x in range(2):
@@ -318,19 +344,23 @@
         copies += [send(g.at[1 - xl, p, (q + k) % 4], r3.at[1, k], to_x[k]) for k in range(4)]
         yield
         arrived(*copies)
-        r4[c, xh] = total(
+        r4[xh] = total(
             g[xl, p, q], *[r3[0, k] for k in range(1, 4)], *[r3[1, k] for k in range(4)]
-        )
-        yield from finish(r4, l, store_in)
-
-    vecs = []
+        ).astype(BF16)
+        yield from finish(r4, r5, l, store_in)
+
+    vecs, leaving = [], []
 
     def store_in(l, half, total):
-        grad_in[l, pl.ds(half * HALF, HALF), :] = total.T
+        s["out_in"][l, pl.ds(half * HALF, HALF), :] = total.T
+        if half == 1:
+            leaving.append(local(s["out_in"].at[l], grad_in.at[l]))
 
     def store_out(l, half, total):
         lanes = pl.ds(half * HALF, HALF)
-        grad_out[l, :, lanes] = total[:R]
+        s["out_out"][l, :, lanes] = total[:R]
+        if half == 1:
+            leaving.append(local(s["out_out"].at[l], grad_out.at[l]))
         if unit_rows(l) > R:
             vec = total[R : R + 8]
             row = lax.broadcasted_iota(jnp.int32, (8, HALF), 0)
@@ -338,8 +368,10 @@
             vecs.append(vec)
             if half == 1:
                 vec = jnp.concatenate(vecs, axis=1)
-                grad_head[...] = (vec * gain_row()).reshape(2 * HALF)
-                grad_gain[...] = (vec * head_row()).reshape(2 * HALF)
+                s["out_head"][...] = (vec * gain_row()).reshape(2 * HALF)
+                s["out_gain"][...] = (vec * head_row()).reshape(2 * HALF)
+                leaving.append(local(s["out_head"], grad_head))
+                leaving.append(local(s["out_gain"], grad_gain))
 
     def go(*jobs):
         for job in jobs:
@@ -491,25 +523,20 @@
         lo = (vec - hi.astype(F32)).astype(BF16)
         s["vec"][...] = jnp.concatenate([hi.astype(F32), lo.astype(F32)], axis=0).astype(BF16)
 
-    def top():
+    def top(j):
         h, g = s["h", LAYERS], s["gb", LAYERS - 1]
-
-        def step(i, carry):
-            row = lax.broadcasted_iota(jnp.int32, (EXTRA, 256), 0)
-            for j in range(4):
-                vec = jnp.dot(s["vec"][...], h[i, j], preferred_element_type=F32)
-                vec = jnp.where(row == 0, vec[:8][0:1] + vec[8:][0:1], 0.0).astype(BF16)
-                g[0, i, j, pl.ds(R, EXTRA)] = vec[:, :HALF]
-                g[1, i, j, pl.ds(R, EXTRA)] = vec[:, HALF:]
-                hg = s["hg"][i, j, 0:1, :]
-                for r in range(0, ROWS, CHUNK):
-                    rows = pl.ds(r, CHUNK)
-                    v = h[i, j, rows, :].astype(F32)
-                    v = lanes2(s["coef"][rows, :]) * hg - v * lanes2(s["tok"][rows, :])
-                    h[i, j, rows, :] = v.astype(BF16)
-            return carry
-
-        lax.fori_loop(0, 4, step, 0)
+        row = lax.broadcasted_iota(jnp.int32, (EXTRA, 256), 0)
+        for i in range(4):
+            vec = jnp.dot(s["vec"][...], h[i, j], preferred_element_type=F32)
+            vec = jnp.where(row == 0, vec[0:1] + vec[8:9], 0.0).astype(BF16)
+            g[0, i, j, pl.ds(R, EXTRA)] = vec[:, :HALF]
+            g[1, i, j, pl.ds(R, EXTRA)] = vec[:, HALF:]
+            hg = s["hg"][i, j, 0:1, :]
+            for r in range(0, ROWS, CHUNK):
+                rows = pl.ds(r, CHUNK)
+                v = h[i, j, rows, :].astype(F32)
+                v = lanes2(s["coef"][rows, :]) * hg - v * lanes2(s["tok"][rows, :])
+                h[i, j, rows, :] = v.astype(BF16)
 
     def back_up(l):
         g, out = s["h", LAYERS], s["da", l]
@@ -523,15 +550,11 @@
 
         lax.fori_loop(0, 4, step, 0)
 
-    def partial(lhs, wide, out):
-        def step(i, carry):
-            for j in range(4):
-                v = jnp.dot(lhs[...], wide[i, j], preferred_element_type=F32).astype(BF16)
-                out[0, i, j, pl.ds(0, R)] = v[:, :HALF]
-                out[1, i, j, pl.ds(0, R)] = v[:, HALF:]
-            return carry
-
-        lax.fori_loop(0, 4, step, 0)
+    def partial(lhs, wide, out, blocks):
+        for i, j in blocks:
+            v = jnp.dot(lhs[...], wide[i, j], preferred_element_type=F32).astype(BF16)
+            out[0, i, j, pl.ds(0, R)] = v[:, :HALF]
+            out[1, i, j, pl.ds(0, R)] = v[:, HALF:]
 
     def inner(l):
         v = s["z_in", l][...]
@@ -561,10 +584,7 @@
 
     in0, in1, in2 = (gather_in(l) for l in range(LAYERS))
     out0, out1, out2 = (gather_out(l) for l in range(LAYERS))
-    go(in0, out0)
-
     core_send, core_recv = s["send"].at[N_SEMS - 1], s["recv"].at[N_SEMS - 1]
-
     def core_copy(src, dst):
         return pltpu.make_async_remote_copy(
             src_ref=src,
@@ -574,7 +594,8 @@
             device_id=to_core,
             device_id_type=MESH,
         )
-
+    go(in0)
+    go(out0)
     def swap_hidden(i, carry):
         yy, zz = i // 4, i % 4
         for xx in range(2):
@@ -584,14 +605,22 @@
                 s["h", 0].at[yy * c + zz * other, zz * c + yy * other, my_rows, pl.ds(xx * HALF, HALF)],
             ).start()
         return carry
-
     lax.fori_loop(0, 16, swap_hidden, 0)
-    s["packs"][c, 2:3, :] = seg_ids[...].astype(F32)
-    s["packs"][c, 3:5, 0:8] = ranks[0].astype(F32)
+    go(in1)
+    go(out1)
+    for copy in local_small:
+        copy.wait()
+    go(in2)
+    go(out2)
+    s["packs"][c, 2:3, :] = s["seg"][...].astype(F32)
+    s["packs"][c, 3:5, 0:8] = s["ranks"][0].astype(F32)
     packs = send(s["packs"].at[c], s["packs"].at[c], to_core)
-
-    go(in1, out1, in2, out2)
-    go(in0, out0, in1, out1, in2, out2)
+    go(in0)
+    go(out0)
+    go(in1)
+    go(out1)
+    go(in2)
+    go(out2)
     block = s["h", 0].at[:, :, my_rows]
     pltpu.make_async_copy(block, block, hidden_sem).wait()
     swapped = core_copy(block, s["h", 0].at[:, :, their_rows])
@@ -599,19 +628,26 @@
     swapped.wait_send()
     squares(0)
     sq = send(s["sq", 0], s["sq_in", 0], to_core)
-    go(in0, out0, in1, out1)
+    go(in0)
+    go(out0)
+    go(in1)
+    go(out1)
     arrived(sq)
     inverse(0)
-    go(out0, in0)
+    go(out0)
+    go(in0)
     down(0)
     zc = send(s["z", 0], s["z_in", 0], to_core)
-    go(out1, in2, out2)
+    go(out1)
+    go(in2)
+    go(out2)
     arrived(zc)
     activate(0)
     go(out0)
     up(0)
     sq = send(s["sq", 1], s["sq_in", 1], to_core)
-    go(in1, out2)
+    go(in1)
+    go(out2)
     down(1)
     zc = send(s["z", 1], s["z_in", 1], to_core)
     arrived(sq)
@@ -624,10 +660,10 @@
     go(in2)
     down(2)
     zc = send(s["z", 2], s["z_in", 2], to_core)
+    go(out2)
+    gains()
     arrived(sq)
     inverse(2)
-    go(out2)
-    gains()
     arrived(zc)
     activate(2)
     up(2)
@@ -637,54 +673,73 @@
     inverse(3)
     arrived(qc)
     head()
-    top()
-
+    out2 = scatter_out(2)
+    go(out2)
     back_up(2)
     dc = send(s["da", 2], s["da_in", 2], to_core)
-    partial(s["act_t", 2], s["h", LAYERS], s["gb", 2])
-    out2 = scatter_out(2)
-    go(out2)
     arrived(dc)
     inner(2)
-    partial(s["dzr_t"], s["h", 2], s["ga", 2])
     in2 = scatter_in(2)
     go(in2)
     back_down(2)
     go(out2)
     back_up(1)
     dc = send(s["da", 1], s["da_in", 1], to_core)
-    partial(s["act_t", 1], s["h", LAYERS], s["gb", 1])
     out1 = scatter_out(1)
-    go(out1, in2, out2)
+    go(out1)
+    go(in2)
+    go(out2)
     arrived(dc)
     inner(1)
-    partial(s["dzr_t"], s["h", 1], s["ga", 1])
     in1 = scatter_in(1)
-    go(in1, out1)
+    go(in1)
+    go(out1)
     back_down(1)
-    go(in2, out2)
+    go(in2)
+    go(out2)
     back_up(0)
     dc = send(s["da", 0], s["da_in", 0], to_core)
-    partial(s["act_t", 0], s["h", LAYERS], s["gb", 0])
     out0 = scatter_out(0)
-    go(out0, in1, out1)
+    go(out0)
+    go(in1)
+    go(out1)
     arrived(dc)
     inner(0)
-    partial(s["dzr_t"], s["h", 0], s["ga", 0])
     in0 = scatter_in(0)
-    go(in0, out0, in2, out2, in1, out1)
-    go(in0, out0, in2, out2, in1, out1)
-    go(in0, out0, in1, out1)
-    go(in0, out0)
-    go(in0, out0)
+    go(in0)
+    go(out0)
+    go(out2)
+    go(in1)
+    go(out1)
+    go(in0)
+    go(out0)
+    go(in2)
+    go(out2)
+    go(in1)
+    go(in2)
+    go(out1)
+    go(out2)
+    go(in0)
+    go(out0)
+    go(in1)
+    go(in2)
+    go(out1)
+    go(in0)
+    go(out0)
+    go(in1)
+    go(out1)
+    go(in0)
+    go(out0)
+    go(in0)
+    go(out0)
     for copy in started:
         copy.wait_send()
-
+    for copy in leaving:
+        copy.wait()
 
 def deliver(*refs):
     for i in range(4):
         refs[i + 4][...] = refs[i][...]
-
 
 def body(hidden, seg_ids, ranks, adapter_in, adapter_out, score_head, final_gain):
     vmem = pl.BlockSpec(memory_space=pltpu.VMEM)
@@ -698,8 +753,8 @@
     grads = pl.pallas_call(
         kernel,
         out_shape=shapes,
-        in_specs=[hbm, vmem, vmem, hbm, hbm, vmem, vmem],
-        out_specs=(vmem,) * 4,
+        in_specs=[hbm] * 7,
+        out_specs=(hbm,) * 4,
         scratch_shapes=list(scratch().values()),
         compiler_params=pltpu.CompilerParams(
             collective_id=0, has_side_effects=True, vmem_limit_bytes=60 * 1024 * 1024
@@ -713,7 +768,6 @@
         out_specs=(vmem,) * 4,
         name="deliver",
     )(*grads)
-
 
 def solution(mesh):
     placed = (

time: 116 us -> 106 us (0.914)
  Pallas kernels: 116 us -> 105 us
    pallas_call x1, Pallas kernels: 114 us -> 103 us  [body(): pl.pallas_call(kernel, out_shape=shapes, in_specs=[hbm] * 7, out_specs=(h...]
where the time goes in v3:
time: 106 us; the launch traced here: 105 us
  Pallas kernels  105 us (99%)
    pallas_call x1, Pallas kernels, body(): pl.pallas_call(kernel, out_shape=shapes, in_specs=[hbm] * 7, out_specs=(h...  103 us

profile of v3, /device:TPU:1, one launch (start us, length us, event | category | flops | bytes accessed | tf_op | source)
XLA Modules:
  0.0 105.5 jit_solution(5725115852250221384)
XLA Ops:
  0.6 102.8 %adapters.1 = (f32[3,256,128]{2,1,0:T(8,128)}, f32[3,128,256]{2,1,0:T(8,128)}, f32[256]{0:T(256)}, f32[256]{0:T(256)}) custom-call(bf16[256,8192]{1,0:T(8,128)(2,1)} %hidden.1, s32[1,256]{1,0:T(1,128)} %seg_ids.1, s32[1,2,8]{2,1,0:T(2,128)} %ranks.1, bf16[3,256,128]{2,1,0:T(8,128)(2,1)} %w_in.1, bf16[3,128,256]{2,1,0:T(8,128)(2,1)} %w_out.1, ...), custom_call_target="tpu_custom_call" | custom-call | tf_op jit(solution)/shard_map/adapters/pallas_call | solution.py:753
  103.4 2.0 %deliver.1 = (f32[3,256,128]{2,1,0:T(8,128)}, f32[3,128,256]{2,1,0:T(8,128)}, f32[256]{0:T(256)}, f32[256]{0:T(256)}) custom-call(f32[3,256,128]{2,1,0:T(8,128)} %get-tuple-element.8.refs_0_, f32[3,128,256]{2,1,0:T(8,128)} %get-tuple-element.9.refs_1_, f32[256]{0:T(256)} %get-tuple-element.10.refs_2_, f32[256]{0:T(256)} %get-tuple-element.11.refs_3_), custom_call_target="tpu_custom_call" | custom-call | tf_op jit(solution)/shard_map/deliver/pallas_call | solution.py:764

commit v4 on v3

--- a/solution.py
+++ b/solution.py
@@ -46,6 +46,7 @@
         shapes["ga3", layer] = pltpu.VMEM((2, 4, R, HALF), BF16)
         shapes["ga4", layer] = pltpu.VMEM((2, R, HALF), BF16)
         shapes["ga5", layer] = pltpu.VMEM((2, R, HALF), F32)
+        shapes["ga6", layer] = pltpu.VMEM((2, R, HALF), BF16)
         shapes["gb", layer] = pltpu.VMEM((2, 4, 4, rows, HALF), BF16)
         shapes["gb1", layer] = pltpu.VMEM((4, 4, rows, HALF), BF16)
         shapes["gb2", layer] = pltpu.VMEM((4, rows, HALF), BF16)
@@ -53,6 +54,7 @@
         shapes["gb4", layer] = pltpu.VMEM((3, rows, HALF), BF16)
         shapes["gb5", layer] = pltpu.VMEM((2, rows, HALF), BF16)
         shapes["gb6", layer] = pltpu.VMEM((2, rows, HALF), F32)
+        shapes["gb7", layer] = pltpu.VMEM((2, rows, HALF), BF16)
     shapes["act"] = pltpu.VMEM((ROWS, R), BF16)
     shapes["dzr"] = pltpu.VMEM((ROWS, R), BF16)
     shapes["dzr_t"] = pltpu.VMEM((R, ROWS), BF16)
@@ -102,6 +104,7 @@
     to_xm = [device(3, 0, by) for by in range(4)]
     to_core = (xh * 2 + other, shard)
     to_rep = ((1 - xh) * 2 + c, shard)
+    to_both = ((1 - xh) * 2 + other, shard)
     to_x = to_xp[:2] + to_xm[2:]
 
     used = [0, 0]
@@ -142,7 +145,7 @@
         return s["gain"][...].astype(F32).reshape(1, 2 * HALF)
 
     barrier = pltpu.get_barrier_semaphore()
-    partners = (*to_p, *to_q, *to_xp, *to_xm, to_core, to_rep)
+    partners = (*to_p, *to_q, *to_xp, *to_xm, to_core, to_rep, to_both)
     for partner in partners:
         pl.semaphore_signal(barrier, inc=1, device_id=partner, device_id_type=MESH)
 
@@ -180,10 +183,17 @@
 
     def gather_in(l):
         w, src = s["wa", l], w_in.at[l, mine]
-        copies = [send(src, w.at[p, q, xl], to) for to in (*to_q, *to_x)]
+        copies = [send(src, w.at[p, q, xl], to) for to in (to_q if l else (*to_q, *to_x))]
         yield
         local_in[l].wait()
         arrived(*copies)
+        if l:
+            copies = [
+                send(w.at[p, low, xl], w.at[p, low, xl], to_xp[0]),
+                send(w.at[p, high, xl], w.at[p, high, xl], to_xm[0]),
+            ]
+            yield
+            arrived(*copies)
         a = send(w.at[p, low], w.at[p, low], to_p[0])
         b = send(w.at[p, high], w.at[p, high], to_p[2])
         copies = [
@@ -255,21 +265,26 @@
             value = value + part.astype(F32)
         return value
 
-    def finish(own, whole, l, store):
-        copy = send(own.at[xh], own.at[xh], to_rep)
-        yield
-        arrived(copy)
+    def finish(own, whole, far, l, store):
+        copies = [send(own.at[xh], own.at[xh], to_rep)]
+        if l == 0:
+            copies += [send(own.at[xh], far.at[xh], to) for to in (to_core, to_both)]
+        yield
+        arrived(*copies)
         whole[c] = total(own[0], own[1])
-        copy = send(whole.at[c], whole.at[c], to_core)
-        yield
-        arrived(copy)
+        if l == 0:
+            whole[other] = total(far[0], far[1])
+        else:
+            copy = send(whole.at[c], whole.at[c], to_core)
+            yield
+            arrived(copy)
         for half in range(2):
             store(l, half, whole[half])
         yield
 
     def scatter_out(l):
         g = s["gb", l]
-        r1, r2, r3, r4, r5, r6 = (s["gb%d" % i, l] for i in range(1, 7))
+        r1, r2, r3, r4, r5, r6, r7 = (s["gb%d" % i, l] for i in range(1, 8))
         across = []
         for j in (q2, qp, qm, q):
             if l == LAYERS - 1:
@@ -310,11 +325,11 @@
         yield
         arrived(*copies)
         r5[xh] = total(g[xl, p, q], r4[0], r4[1], r4[2]).astype(BF16)
-        yield from finish(r5, r6, l, store_out)
+        yield from finish(r5, r6, r7, l, store_out)
 
     def scatter_in(l):
         g = s["ga", l]
-        r1, r2, r3, r4, r5 = (s["ga%d" % i, l] for i in range(1, 6))
+        r1, r2, r3, r4, r5, r6 = (s["ga%d" % i, l] for i in range(1, 7))
         partial(s["dzr_t"], s["h", l], g, [(p2, j) for j in range(4)])
         a = send(g.at[:, p2, low], r1.at[:, low], to_p[0])
         b = send(g.at[:, p2, high], r1.at[:, high], to_p[2])
@@ -347,7 +362,7 @@
         r4[xh] = total(
             g[xl, p, q], *[r3[0, k] for k in range(1, 4)], *[r3[1, k] for k in range(4)]
         ).astype(BF16)
-        yield from finish(r4, r5, l, store_in)
+        yield from finish(r4, r5, r6, l, store_in)
 
     vecs, leaving = [], []
 
@@ -621,6 +636,9 @@
     go(out1)
     go(in2)
     go(out2)
+    go(in0)
+    go(out0)
+    go(in1)
     block = s["h", 0].at[:, :, my_rows]
     pltpu.make_async_copy(block, block, hidden_sem).wait()
     swapped = core_copy(block, s["h", 0].at[:, :, their_rows])
@@ -628,18 +646,16 @@
     swapped.wait_send()
     squares(0)
     sq = send(s["sq", 0], s["sq_in", 0], to_core)
-    go(in0)
-    go(out0)
-    go(in1)
-    go(out1)
+    go(out1)
+    go(in2)
     arrived(sq)
     inverse(0)
     go(out0)
     go(in0)
     down(0)
     zc = send(s["z", 0], s["z_in", 0], to_core)
-    go(out1)
-    go(in2)
+    go(in1)
+    go(out1)
     go(out2)
     arrived(zc)
     activate(0)
@@ -647,6 +663,7 @@
     up(0)
     sq = send(s["sq", 1], s["sq_in", 1], to_core)
     go(in1)
+    go(in2)
     go(out2)
     down(1)
     zc = send(s["z", 1], s["z_in", 1], to_core)
@@ -660,12 +677,12 @@
     go(in2)
     down(2)
     zc = send(s["z", 2], s["z_in", 2], to_core)
-    go(out2)
-    gains()
     arrived(sq)
     inverse(2)
     arrived(zc)
     activate(2)
+    go(out2)
+    gains()
     up(2)
     sq = send(s["sq", 3], s["sq_in", 3], to_core)
     qc = send(s["q"], s["q_in"], to_core)

time: 106 us -> 101 us (0.953)
  Pallas kernels: 105 us -> 99.8 us
    pallas_call x1, Pallas kernels: 103 us -> 97.8 us  [body(): pl.pallas_call(kernel, out_shape=shapes, in_specs=[hbm] * 7, out_specs=(h...]
where the time goes in v4:
time: 101 us; the launch traced here: 100 us
  Pallas kernels  99.8 us (99%)
    pallas_call x1, Pallas kernels, body(): pl.pallas_call(kernel, out_shape=shapes, in_specs=[hbm] * 7, out_specs=(h...  97.8 us
    pallas_call x1, Pallas kernels, body(): pl.pallas_call(deliver, out_shape=shapes, in_specs=[vmem] * 4, out_specs=...  2.03 us

profile of v4, /device:TPU:1, one launch (start us, length us, event | category | flops | bytes accessed | tf_op | source)
XLA Modules:
  0.0 100.4 jit_solution(10727987102976245082)
XLA Ops:
  0.6 97.8 %adapters.1 = (f32[3,256,128]{2,1,0:T(8,128)}, f32[3,128,256]{2,1,0:T(8,128)}, f32[256]{0:T(256)}, f32[256]{0:T(256)}) custom-call(bf16[256,8192]{1,0:T(8,128)(2,1)} %hidden.1, s32[1,256]{1,0:T(1,128)} %seg_ids.1, s32[1,2,8]{2,1,0:T(2,128)} %ranks.1, bf16[3,256,128]{2,1,0:T(8,128)(2,1)} %w_in.1, bf16[3,128,256]{2,1,0:T(8,128)(2,1)} %w_out.1, ...), custom_call_target="tpu_custom_call" | custom-call | tf_op jit(solution)/shard_map/adapters/pallas_call | solution.py:770
  98.4 2.0 %deliver.1 = (f32[3,256,128]{2,1,0:T(8,128)}, f32[3,128,256]{2,1,0:T(8,128)}, f32[256]{0:T(256)}, f32[256]{0:T(256)}) custom-call(f32[3,256,128]{2,1,0:T(8,128)} %get-tuple-element.8.refs_0_, f32[3,128,256]{2,1,0:T(8,128)} %get-tuple-element.9.refs_1_, f32[256]{0:T(256)} %get-tuple-element.10.refs_2_, f32[256]{0:T(256)} %get-tuple-element.11.refs_3_), custom_call_target="tpu_custom_call" | custom-call | tf_op jit(solution)/shard_map/deliver/pallas_call | solution.py:781

commit v5 on v4

--- a/solution.py
+++ b/solution.py
@@ -755,11 +755,29 @@
         copy.wait()
 
 def deliver(*refs):
-    for i in range(4):
-        refs[i + 4][...] = refs[i][...]
+    came, went = refs[-2], refs[-1]
+    pieces = [(i, l) for l in range(LAYERS) for i in range(2)] + [(2, None), (3, None)]
+
+    def part(ref, l):
+        return ref if l is None else ref.at[l]
+
+    reads = [
+        pltpu.make_async_copy(part(refs[i], l), part(refs[i + 8], l), came.at[k])
+        for k, (i, l) in enumerate(pieces)
+    ]
+    writes = [
+        pltpu.make_async_copy(part(refs[i + 8], l), part(refs[i + 4], l), went.at[k])
+        for k, (i, l) in enumerate(pieces)
+    ]
+    for copy in reads:
+        copy.start()
+    for read, write in zip(reads, writes):
+        read.wait()
+        write.start()
+    for copy in writes:
+        copy.wait()
 
 def body(hidden, seg_ids, ranks, adapter_in, adapter_out, score_head, final_gain):
-    vmem = pl.BlockSpec(memory_space=pltpu.VMEM)
     hbm = pl.BlockSpec(memory_space=pl.ANY)
     shapes = (
         jax.ShapeDtypeStruct((LAYERS, 2 * HALF, R), F32),
@@ -781,8 +799,11 @@
     return pl.pallas_call(
         deliver,
         out_shape=shapes,
-        in_specs=[vmem] * 4,
-        out_specs=(vmem,) * 4,
+        in_specs=[hbm] * 4,
+        out_specs=(hbm,) * 4,
+        scratch_shapes=[pltpu.VMEM(x.shape, x.dtype) for x in shapes]
+        + [pltpu.SemaphoreType.DMA((8,)), pltpu.SemaphoreType.DMA((8,))],
+        compiler_params=pltpu.CompilerParams(vmem_limit_bytes=60 * 1024 * 1024),
         name="deliver",
     )(*grads)
 

time: 101 us -> 101 us (level)
  no operation moved by 1% of the time
where the time goes in v5:
time: 101 us
  Pallas kernels  99.8 us (99%)
    pallas_call x1, Pallas kernels, body(): pl.pallas_call(kernel, out_shape=shapes, in_specs=[hbm] * 7, out_specs=(h...  97.8 us

profile of v5, /device:TPU:1, one launch (start us, length us, event | category | flops | bytes accessed | tf_op | source)
XLA Modules:
  0.0 100.6 jit_solution(18302457516314102933)
XLA Ops:
  0.6 97.8 %adapters.1 = (f32[3,256,128]{2,1,0:T(8,128)}, f32[3,128,256]{2,1,0:T(8,128)}, f32[256]{0:T(256)}, f32[256]{0:T(256)}) custom-call(bf16[256,8192]{1,0:T(8,128)(2,1)} %hidden.1, s32[1,256]{1,0:T(1,128)} %seg_ids.1, s32[1,2,8]{2,1,0:T(2,128)} %ranks.1, bf16[3,256,128]{2,1,0:T(8,128)(2,1)} %w_in.1, bf16[3,128,256]{2,1,0:T(8,128)(2,1)} %w_out.1, ...), custom_call_target="tpu_custom_call" | custom-call | tf_op jit(solution)/shard_map/adapters/pallas_call | solution.py:788
  98.4 2.0 %deliver.1 = (f32[3,256,128]{2,1,0:T(8,128)}, f32[3,128,256]{2,1,0:T(8,128)}, f32[256]{0:T(256)}, f32[256]{0:T(256)}) custom-call(f32[3,256,128]{2,1,0:T(8,128)} %get-tuple-element.8.refs_0_, f32[3,128,256]{2,1,0:T(8,128)} %get-tuple-element.9.refs_1_, f32[256]{0:T(256)} %get-tuple-element.10.refs_2_, f32[256]{0:T(256)} %get-tuple-element.11.refs_3_), custom_call_target="tpu_custom_call" | custom-call | tf_op jit(solution)/shard_map/deliver/pallas_call | solution.py:799
